TPU v7x, 256 devices: a whole 4x4x8 slice. The times are simulated.
256 devices in a mesh: ctx: 64 (over x_lo, z, y), tp: 4 (over x_hi, core).
Axes of the slice: x: 4 (x_hi: 2, x_lo: 2; x = x_hi * 2 + x_lo), y: 4, z: 8, core: 2. Of those that a mesh axis runs over, the one named last changes fastest.
Arguments:
- queries: bfloat16 [8192, 4096], P('ctx', 'tp'), may hold values from -64 to 64
- keys: bfloat16 [8192, 1024], P('ctx', 'tp'), may hold values from -4 to 4
- values: bfloat16 [8192, 1024], P('ctx', 'tp'), may hold values from -6 to 6
- grad_out: bfloat16 [8192, 4096], P('ctx', 'tp'), may hold values from -6 to 6
- out_weight: bfloat16 [4096, 4096], P(None, 'tp'), may hold values from -0.09375 to 0.09375
- segments: int32 [8192], P('ctx'), may hold values from 0 to 1, as said below
Outputs:
- query_grad: bfloat16 [8192, 4096], P('ctx', 'tp')
- key_gradient: bfloat16 [8192, 1024], P('ctx', 'tp')
- value_gradient: bfloat16 [8192, 1024], P('ctx', 'tp')
Inputs may be any that keep to these rules, and one draw needn't show every extreme that they name: `segments`: document numbers never fall along the tokens, start at 0, and every document starts at a multiple of 8 tokens; there are exactly 2 documents.
All inputs are finite; a program needn't handle non-finite values.
Results may differ from a plain program's by a relative error of at most 0.015.
Values may be sent and summed in bfloat16 or wider, within the bound.
No kernel may reach another device: no remote copies, remote signals or barrier semaphores. Data moves between devices by JAX's collectives and lax.ppermute only.
A program may use at most 128 MiB of HBM per device.

v0:
```python
import jax
import jax.numpy as jnp
from jax import lax
from jax.sharding import PartitionSpec as P

QUERY_HEADS = 32
KEY_VALUE_HEADS = 8
HEAD_SIZE = 128


def per_device(queries, keys, values, grad_out, out_weight, segments):
    rows = queries.shape[0]
    groups = keys.shape[1] // HEAD_SIZE
    group_ratio = QUERY_HEADS // KEY_VALUE_HEADS
    scale = HEAD_SIZE ** (-0.5)
    first = lax.axis_index("ctx") * rows
    qpos = first + jnp.arange(rows, dtype=jnp.int32)
    last_pos = first + rows - 1
    first_seg = segments[0]
    upstream_wide = jnp.dot(
        lax.all_gather(grad_out, "tp", axis=1, tiled=True),
        out_weight,
        preferred_element_type=jnp.float32,
    )
    upstream = upstream_wide.astype(jnp.bfloat16).reshape(rows, groups, group_ratio, HEAD_SIZE)
    query_four = queries.reshape(rows, groups, group_ratio, HEAD_SIZE)
    all_keys, all_values, all_segs = (
        lax.all_gather(keys, "ctx", axis=0, tiled=True),
        lax.all_gather(values, "ctx", axis=0, tiled=True),
        lax.all_gather(segments, "ctx", axis=0, tiled=True),
    )
    total = all_keys.shape[0]
    width = min(512, total)
    blocks = total // width

    def block_at(index):
        start = index * width
        key_blk = lax.dynamic_slice_in_dim(all_keys, start, width, 0).reshape(
            width, groups, HEAD_SIZE
        )
        value_blk = lax.dynamic_slice_in_dim(all_values, start, width, 0).reshape(
            width, groups, HEAD_SIZE
        )
        seg_blk = lax.dynamic_slice_in_dim(all_segs, start, width, 0)
        kpos = start + jnp.arange(width, dtype=jnp.int32)
        allowed = (kpos[None, :] <= qpos[:, None]) & (seg_blk[None, :] == segments[:, None])
        needed = (start <= last_pos) & (seg_blk[width - 1] >= first_seg)
        return (start, key_blk, value_blk, allowed, needed)

    def block_scores(key_blk, value_blk, allowed):
        scores = (
            jnp.einsum("qgrd,kgd->grqk", query_four, key_blk, preferred_element_type=jnp.float32)
            * scale
        )
        scores = jnp.where(allowed[None, None], scores, jnp.float32(-1e30))
        dprobs = jnp.einsum(
            "qgrd,kgd->grqk", upstream, value_blk, preferred_element_type=jnp.float32
        )
        return (scores, dprobs)

    def statistics(index, carry):
        start, key_blk, value_blk, allowed, needed = block_at(index)

        def statistics_update(state):
            top_old, mass, weighted = state
            scores, dprobs = block_scores(key_blk, value_blk, allowed)
            top_new = jnp.maximum(top_old, jnp.max(scores, axis=-1))
            probs = jnp.where(allowed[None, None], jnp.exp(scores - top_new[..., None]), 0.0)
            factor = jnp.exp(top_old - top_new)
            mass = mass * factor + jnp.sum(probs, axis=-1)
            weighted = weighted * factor + jnp.sum(probs * dprobs, axis=-1)
            return (top_new, mass, weighted)

        return lax.cond(needed, statistics_update, lambda state: state, carry)

    start_state = (
        jnp.full((groups, group_ratio, rows), -1e30, jnp.float32),
        jnp.zeros((groups, group_ratio, rows), jnp.float32),
        jnp.zeros((groups, group_ratio, rows), jnp.float32),
    )
    top, mass, weighted = lax.fori_loop(0, blocks, statistics, start_state)
    lse = top + jnp.log(mass)
    delta = weighted / mass

    def gradients(index, carry):
        start, key_blk, value_blk, allowed, needed = block_at(index)

        def gradients_update(state):
            query_acc, key_acc, value_acc = state
            scores, dprobs = block_scores(key_blk, value_blk, allowed)
            probs = jnp.where(allowed[None, None], jnp.exp(scores - lse[..., None]), 0.0)
            dscores = probs * (dprobs - delta[..., None])
            probs_low = probs.astype(jnp.bfloat16)
            dscores_low = dscores.astype(jnp.bfloat16)
            query_acc = query_acc + jnp.einsum(
                "grqk,kgd->qgrd", dscores_low, key_blk, preferred_element_type=jnp.float32
            )
            key_term = (
                jnp.einsum(
                    "grqk,qgrd->kgd", dscores_low, query_four, preferred_element_type=jnp.float32
                )
                * scale
            )
            value_term = jnp.einsum(
                "grqk,qgrd->kgd", probs_low, upstream, preferred_element_type=jnp.float32
            )
            key_acc = lax.dynamic_update_slice_in_dim(
                key_acc, key_term.reshape(width, groups * HEAD_SIZE), start, 0
            )
            value_acc = lax.dynamic_update_slice_in_dim(
                value_acc, value_term.reshape(width, groups * HEAD_SIZE), start, 0
            )
            return (query_acc, key_acc, value_acc)

        return lax.cond(needed, gradients_update, lambda state: state, carry)

    empty_terms = jnp.zeros((total, groups * HEAD_SIZE), jnp.float32)
    grad_state = (
        jnp.zeros((rows, groups, group_ratio, HEAD_SIZE), jnp.float32),
        empty_terms,
        empty_terms,
    )
    query_acc, key_terms, value_terms = lax.fori_loop(0, blocks, gradients, grad_state)
    query_grad = (
        (query_acc * scale).reshape(rows, groups * group_ratio * HEAD_SIZE).astype(jnp.bfloat16)
    )
    key_sum, value_sum = (
        lax.psum_scatter(key_terms, "ctx", scatter_dimension=0, tiled=True),
        lax.psum_scatter(value_terms, "ctx", scatter_dimension=0, tiled=True),
    )
    return (query_grad, key_sum.astype(jnp.bfloat16), value_sum.astype(jnp.bfloat16))


def solution(mesh):
    in_specs = (
        P("ctx", "tp"),
        P("ctx", "tp"),
        P("ctx", "tp"),
        P("ctx", "tp"),
        P(None, "tp"),
        P("ctx"),
    )
    out_specs = (P("ctx", "tp"), P("ctx", "tp"), P("ctx", "tp"))
    return jax.shard_map(
        per_device, mesh=mesh, in_specs=in_specs, out_specs=out_specs, check_vma=False
    )
```

profile of v0, /device:TPU:2, one launch (start us, length us, event | category | flops | bytes accessed | tf_op | source)
XLA Modules:
  0.0 1344.6 jit_solution(7224552372082858660)
XLA Ops:
  7.2 0.7 all-gather.9.cloned.1.call-update
  7.9 1.6 copy.50
  9.6 1.6 copy.52
  11.2 1.1 copy.51
  12.6 157.5 %all-gather = s32[64,1,128]{2,1,0:T(1,128)S(1)} all-gather(s32[1,1,128]{2,1,0:T(1,128)} %bitcast.132), channel_id=1, replica_groups=mesh['ctx'=64,'tp'=4] {'ctx'}, dimensions={0}, use_global_device_ids=true | all-gather | bytes 33280 | tf_op jit(solution)/shard_map/all_gather | solution.py:30
  170.1 5.0 convolution_convert_fusion
  175.5 105.6 %all-gather.5.cloned.1.call-done = bf16[8192,256]{0,1:T(8,128)(2,1)} async-done(((bf16[128,256]{0,1:T(8,128)(2,1)}), bf16[8192,256]{0,1:T(8,128)(2,1)}) %all-gather.5.cloned.1.call-update) | async-done | bytes 4194320 | tf_op jit(solution)/shard_map/all_gather | solution.py:28
  281.1 243.8 %all-gather.7.cloned.1.call-done = bf16[8192,256]{0,1:T(8,128)(2,1)} async-done(((bf16[128,256]{0,1:T(8,128)(2,1)}), bf16[8192,256]{0,1:T(8,128)(2,1)}) %all-gather.7.cloned.1.call-update) | async-done | bytes 4194320 | tf_op jit(solution)/shard_map/all_gather | solution.py:29
  525.0 30.6 %while.36 = (s32[]{:T(128)}, f32[2,4,128]{2,1,0:T(4,128)S(1)}, f32[2,4,128]{2,1,0:T(4,128)S(1)}, f32[2,4,128]{2,1,0:T(4,128)S(1)}, s32[]{:T(128)}, /*index=5*/s3...) while((s32[]{:T(128)}, f32[2,4,128]{2,1,0:T(4,128)S(1)}, ...), condition=%wide.region_6.7_spmd.clone, body=%wide.region_0.6_spmd.clone.sunk | while | flops 275975808 | bytes 8741797 | solution.py:81
  534.1 3.3 conditional.6
  534.4 1.1 constant_dynamic-slice_fusion
  536.0 0.8 fusion.4
  538.7 3.3 conditional.6
  538.9 1.1 constant_dynamic-slice_fusion
  540.5 0.8 fusion.4
  543.2 3.3 conditional.6
  543.5 1.1 constant_dynamic-slice_fusion
  545.1 0.8 fusion.4
  555.7 4.2 broadcast_in_dim.89.clone
  559.9 4.2 broadcast_in_dim.89
  564.1 40.9 %while.37 = (s32[]{:T(128)}, f32[128,2,4,128]{3,0,2,1:T(8,128)S(1)}, f32[8192,256]{0,1:T(8,128)}, f32[8192,256]{0,1:T(8,128)}, s32[]{:T(128)}, /*index=5*/s32[81...) while((s32[]{:T(128)}, ...), condition=%wide.region_10.11_spmd.clone, body=%wide.region_7.10_spmd.clone.sunk | while | flops 675742336 | bytes 16671727 | solution.py:123
  565.6 0.6 slice.23
  567.0 0.6 slice.23
  574.0 6.1 conditional.7
  574.2 1.0 constant_dynamic-slice_fusion.3
  575.2 1.0 constant_dynamic-slice_fusion.2
  576.2 0.7 fusion.11
  578.4 0.6 fusion.13
  579.0 1.1 constant_dynamic-update-slice_fusion
  581.4 6.2 conditional.7
  581.7 1.0 constant_dynamic-slice_fusion.3
  582.7 1.0 constant_dynamic-slice_fusion.2
  583.7 0.7 fusion.11
  585.9 0.6 fusion.13
  586.5 1.1 constant_dynamic-update-slice_fusion
  588.9 6.2 conditional.7
  589.2 1.0 constant_dynamic-slice_fusion.3
  590.2 1.0 constant_dynamic-slice_fusion.2
  591.2 0.7 fusion.11
  593.4 0.6 fusion.13
  594.0 1.1 constant_dynamic-update-slice_fusion
  605.0 9.0 copy.58
  614.1 9.0 copy.57
  623.4 0.9 convert_element_type.41
  624.3 384.8 %reduce-scatter.5.cloned.1.call-done = f32[128,256]{1,0:T(8,128)} async-done(((f32[8192,256]{1,0:T(8,128)}), f32[128,256]{1,0:T(8,128)}) %reduce-scatter.5.cloned.1.call-update) | async-done | bytes 131088 | tf_op jit(solution)/shard_map/reduce_scatter | solution.py:129
  1009.0 1.5 convert_element_type.43
  1010.6 325.9 %reduce-scatter.3.cloned.1.call-done = f32[128,256]{1,0:T(8,128)} async-done(((f32[8192,256]{1,0:T(8,128)}), f32[128,256]{1,0:T(8,128)}) %reduce-scatter.3.cloned.1.call-update) | async-done | bytes 131088 | tf_op jit(solution)/shard_map/reduce_scatter | solution.py:128
  1336.5 1.5 convert_element_type.42
  (217 shorter events, 31.0 us)
Async XLA Ops:
  7.2 162.9 %all-gather.9.cloned.1.call-start = ((), (), s32[]{:S(2)}) async-start(), calls=%async_computation.4 | async-start | bytes 1310720 | tf_op jit(solution)/shard_map/all_gather | solution.py:21
  7.9 273.2 %all-gather.5.cloned.1.call-start = ((), (), s32[]{:S(2)}) async-start(), calls=%async_computation.2 | async-start | bytes 4259840 | tf_op jit(solution)/shard_map/all_gather | solution.py:28
  9.5 515.4 %all-gather.7.cloned.1.call-start = ((), (), s32[]{:S(2)}) async-start(), calls=%async_computation.3 | async-start | bytes 4259840 | tf_op jit(solution)/shard_map/all_gather | solution.py:29
  11.2 997.8 %reduce-scatter.5.cloned.1.call-start = ((), (), s32[]{:S(2)}) async-start(), calls=%async_computation.6 | async-start | bytes 8519680 | tf_op jit(solution)/shard_map/reduce_scatter | solution.py:129
  170.1 354.9 %copy-start = (s32[128]{0:T(128)S(1)}, s32[128]{0:T(128)}, u32[]{:S(2)}) copy-start(s32[128]{0:T(128)} %param.19) | copy-start | bytes 1540
  614.0 722.4 %reduce-scatter.3.cloned.1.call-start = ((), (), s32[]{:S(2)}) async-start(), calls=%async_computation.5 | async-start | bytes 8519680 | tf_op jit(solution)/shard_map/reduce_scatter | solution.py:128
Sparse Core Ops, SparseCore 0:
  9.8 25.3 all-gather.8
  37.5 243.6 all-gather.4
  283.4 241.4 all-gather.6
  614.2 394.8 reduce-scatter.4
  1011.4 325.0 reduce-scatter.2
where the time goes:
time: 1350 us; the launch traced here: 1340 us
  waiting for transfers between devices  1060 us (79%)
  blocking collectives  157 us (12%)
  local copies, waits for them, and re-layouts  66.5 us (5%)
  loops' own time  22 us (2%)
  matrix products  17.6 us (1%)
  between operations  13.9 us (1%)
    reduce_scatter x1, waiting for transfers between devices, per_device(): lax.psum_scatter(value_terms, 'ctx', scatter_dimension=0, tiled=True)  385 us
    reduce_scatter x1, waiting for transfers between devices, per_device(): lax.psum_scatter(key_terms, 'ctx', scatter_dimension=0, tiled=True)  326 us
    all_gather x1, waiting for transfers between devices, per_device(): lax.all_gather(values, 'ctx', axis=0, tiled=True)  244 us
    all_gather x1, blocking collectives, per_device(): lax.all_gather(segments, 'ctx', axis=0, tiled=True)  157 us
    all_gather x1, waiting for transfers between devices, per_device(): lax.all_gather(keys, 'ctx', axis=0, tiled=True)  106 us
  transfers between devices with their start and end apart: 5, of which 4 were waited for; matrix products, arithmetic and copies ran while one was open for 2% of the time, Pallas kernels for 0%

commit v1 on v0

v1 whole, which is shorter than its diff:
```python
import functools
import math

import jax
import jax.numpy as jnp
from jax import lax
from jax.experimental import pallas as pl
from jax.experimental.pallas import tpu as pltpu
from jax.sharding import Mesh, PartitionSpec as P

HEAD = 128
RATIO = 4
CHUNK = 128
XL, NZ, NY = 2, 8, 4
HALF = NZ * NY * CHUNK
PLANE = NY * CHUNK
KEYS = XL * NZ * CHUNK
KT = 256
ROWS = 1024
PAIRS = 4
GROUP = RATIO * HEAD
SCALE = HEAD**-0.5
C2 = SCALE * math.log2(math.e)
NEG = -1e30
WIDE = jnp.float32
LOW = jnp.bfloat16
NT = (((1,), (1,)), ((), ()))
NN = (((1,), (0,)), ((), ()))
VMEM_LIMIT = 48 * 1024 * 1024


def dot(a, b, dims=NN):
    return lax.dot_general(a, b, dims, preferred_element_type=WIDE)


def vspec():
    return pl.BlockSpec(memory_space=pltpu.VMEM)


def sspec():
    return pl.BlockSpec(memory_space=pltpu.SMEM)


def params():
    return pltpu.CompilerParams(vmem_limit_bytes=VMEM_LIMIT)


def up_first(pos, own, mate, weight):
    def kernel(pos_ref, g0, g1, w_ref, out_ref):
        @pl.when(pl.program_id(0) == 0)
        def _():
            out_ref[...] = dot(g0[...], w_ref[...])

        @pl.when(pl.program_id(0) == 1)
        def _():
            out_ref[...] += dot(g1[...], w_ref[...])

    full = pl.BlockSpec((CHUNK, 1024), lambda r, pos: (0, 0))
    return pl.pallas_call(
        kernel,
        grid_spec=pltpu.PrefetchScalarGridSpec(
            num_scalar_prefetch=1,
            grid=(2,),
            in_specs=[
                full,
                full,
                pl.BlockSpec((1024, 1024), lambda r, pos: (jnp.bitwise_xor(pos[0], r), 0)),
            ],
            out_specs=pl.BlockSpec((CHUNK, 1024), lambda r, pos: (0, 0)),
        ),
        out_shape=jax.ShapeDtypeStruct((CHUNK, 1024), WIDE),
        compiler_params=params(),
        name="upstream_first",
    )(pos, own, mate, weight)


def up_second(pos, part, far, far_mate, weight):
    def kernel(pos_ref, part_ref, g0, g1, w_ref, own_ref, oth_ref, acc):
        @pl.when(pl.program_id(0) == 0)
        def _():
            acc[...] = part_ref[...] + dot(g0[...], w_ref[...])

        @pl.when(pl.program_id(0) == 1)
        def _():
            acc[...] += dot(g1[...], w_ref[...])
            xl = pos_ref[1]
            own_ref[...] = acc[:, pl.ds(pl.multiple_of(xl * GROUP, GROUP), GROUP)].astype(LOW)
            oth_ref[...] = acc[:, pl.ds(pl.multiple_of((1 - xl) * GROUP, GROUP), GROUP)].astype(LOW)

    full = pl.BlockSpec((CHUNK, 1024), lambda r, pos: (0, 0))
    half = pl.BlockSpec((CHUNK, GROUP), lambda r, pos: (0, 0))
    return pl.pallas_call(
        kernel,
        grid_spec=pltpu.PrefetchScalarGridSpec(
            num_scalar_prefetch=1,
            grid=(2,),
            in_specs=[
                full,
                full,
                full,
                pl.BlockSpec((1024, 1024), lambda r, pos: (jnp.bitwise_xor(pos[0], 2 + r), 0)),
            ],
            out_specs=[half, half],
            scratch_shapes=[pltpu.VMEM((CHUNK, 1024), WIDE)],
        ),
        out_shape=[jax.ShapeDtypeStruct((CHUNK, GROUP), LOW)] * 2,
        compiler_params=params(),
        name="upstream_second",
    )(pos, part, far, far_mate, weight)


def stack_rows(dst, blocks):
    for o in range(2):
        for dy in range(NY):
            for h in range(RATIO):
                start = (dy % 2) * GROUP + h * CHUNK
                dst[o * 2 + dy // 2, start : start + CHUNK, :] = blocks[o][dy][
                    :, h * HEAD : (h + 1) * HEAD
                ]


def key_chunk(xl, z, o, d):
    half = xl if o == 0 else 1 - xl
    return half * NZ + lax.rem(z + d, NZ)


def row_limits(pair, xl, z, y, b):
    o = pair // 2
    h = jnp.where(o == 0, xl, 1 - xl)
    dy0 = (pair % 2) * 2
    y0 = lax.rem(y + dy0, NY)
    y1 = lax.rem(y + dy0 + 1, NY)
    base = h * HALF + z * PLANE
    lane = lax.broadcasted_iota(jnp.int32, (1, ROWS), 1)
    off = jnp.where(lane < GROUP, y0, y1) * CHUNK + jnp.bitwise_and(lane, CHUNK - 1)
    key_base = h * NZ * CHUNK + z * CHUNK
    high = key_base + jnp.clip(off - y * CHUNK + 1, 0, CHUNK)
    bh = b // HALF
    bz = (b - bh * HALF) // PLANE
    cb = (
        bh * NZ * CHUNK
        + bz * CHUNK
        + jnp.clip(b - bh * HALF - bz * PLANE - y * CHUNK, 0, CHUNK)
    )
    low = jnp.where(base + off >= b, cb, 0)
    first = base + jnp.minimum(y0, y1) * CHUNK
    t_low = jnp.where(first >= b, cb // KT, 0)
    top = key_base + jnp.where(jnp.maximum(y0, y1) >= y, CHUNK, 0)
    t_high = (top + KT - 1) // KT
    return low, high, t_low, t_high


def masked_scores(k, q, t, low, high):
    s = dot(k, q, NT) * C2
    kk = t * KT + lax.broadcasted_iota(jnp.int32, (KT, ROWS), 0)
    return jnp.where((kk >= low) & (kk < high), s, NEG)


def forward(scalars, q_blocks, kv_blocks):
    def kernel(sc, *refs):
        q = [refs[0:4], refs[4:8]]
        kv = refs[8:16]
        o_ref, ml_ref, qs, kc, vt = refs[16:]
        xl, z, y, b = sc[0], sc[1], sc[2], sc[3]
        stack_rows(qs, q)
        for d in range(NZ):
            for o in range(2):
                at = key_chunk(xl, z, o, d)
                rows = slice(o * CHUNK, (o + 1) * CHUNK)
                kc[at] = kv[d][rows, :HEAD]
                vt[at, :HEAD, :] = kv[d][rows, HEAD:].T
                vt[at, HEAD:, :] = jnp.ones((16, CHUNK), LOW)

        def one_pair(pair, _):
            low, high, t_low, t_high = row_limits(pair, xl, z, y, b)
            o_ref[pair] = jnp.zeros((HEAD + 16, ROWS), WIDE)
            qp = qs[pair]

            def tile(t, top):
                k = kc[pl.ds(2 * t, 2)].reshape(KT, HEAD)
                s = masked_scores(k, qp, t, low, high)
                new = jnp.maximum(top, jnp.max(s, axis=0, keepdims=True))
                p = jnp.exp2(s - new).astype(LOW)
                v = jnp.concatenate([vt[2 * t], vt[2 * t + 1]], axis=1)
                o_ref[pair] = o_ref[pair] * jnp.exp2(top - new) + dot(v, p)
                return new

            top = lax.fori_loop(t_low, t_high, tile, jnp.full((1, ROWS), NEG, WIDE))
            ml_ref[pl.ds(pair, 1), :] = top
            return 0

        lax.fori_loop(0, PAIRS, one_pair, 0)
        for pair in range(PAIRS):
            ml_ref[PAIRS + pair : PAIRS + pair + 1, :] = o_ref[pair, HEAD : HEAD + 1, :]

    return pl.pallas_call(
        kernel,
        in_specs=[sspec()] + [vspec()] * 16,
        out_specs=[vspec()] * 2,
        out_shape=[
            jax.ShapeDtypeStruct((PAIRS, HEAD + 16, ROWS), WIDE),
            jax.ShapeDtypeStruct((2 * PAIRS, ROWS), WIDE),
        ],
        scratch_shapes=[
            pltpu.VMEM((PAIRS, ROWS, HEAD), LOW),
            pltpu.VMEM((XL * NZ, CHUNK, HEAD), LOW),
            pltpu.VMEM((XL * NZ, HEAD + 16, CHUNK), LOW),
        ],
        compiler_params=params(),
        cost_estimate=pl.CostEstimate(
            flops=8 * 10**9, bytes_accessed=6 * 2**20, transcendentals=4 * 2**20
        ),
        name="forward",
    )(scalars, *q_blocks[0], *q_blocks[1], *kv_blocks)


def weighted(o_part, ml, u_blocks):
    def kernel(o_ref, ml_ref, *refs):
        u = [refs[0:4], refs[4:8]]
        out_ref = refs[8]
        out_ref[: 2 * PAIRS, :] = ml_ref[...]
        for o in range(2):
            for dy in range(NY):
                pair = o * 2 + dy // 2
                for h in range(RATIO):
                    start = (dy % 2) * GROUP + h * CHUNK
                    ut = u[o][dy][:, h * HEAD : (h + 1) * HEAD].astype(WIDE).T
                    part = ut * o_ref[pair, :HEAD, start : start + CHUNK]
                    out_ref[
                        2 * PAIRS + pair : 2 * PAIRS + pair + 1, start : start + CHUNK
                    ] = jnp.sum(part, axis=0, keepdims=True)

    return pl.pallas_call(
        kernel,
        in_specs=[vspec()] * 10,
        out_specs=vspec(),
        out_shape=jax.ShapeDtypeStruct((3 * PAIRS, ROWS), WIDE),
        compiler_params=params(),
        name="weighted",
    )(o_part, ml, *u_blocks[0], *u_blocks[1])


def backward(scalars, stats, q_blocks, u_blocks, kv_blocks):
    def kernel(sc, *refs):
        st = refs[0:4]
        q = [refs[4:8], refs[8:12]]
        u = [refs[12:16], refs[16:20]]
        kv = refs[20:28]
        dq_out = refs[28:32]
        dkv_out = refs[32:40]
        qs, us, kc, vc, kt, dk, dv, dqt, al, lse_s, delta_s = refs[40:]
        xl, z, y, b = sc[0], sc[1], sc[2], sc[3]
        stack_rows(qs, q)
        stack_rows(us, u)
        for d in range(NZ):
            for o in range(2):
                at = key_chunk(xl, z, o, d)
                rows = slice(o * CHUNK, (o + 1) * CHUNK)
                key = kv[d][rows, :HEAD]
                kc[at] = key
                vc[at] = kv[d][rows, HEAD:]
                kt[at] = key.T
        dk[...] = jnp.zeros(dk.shape, WIDE)
        dv[...] = jnp.zeros(dv.shape, WIDE)
        dqt[...] = jnp.zeros(dqt.shape, WIDE)

        for i in range(NY):
            for row in range(0, 3 * PAIRS, 2):
                for dy in range(NY):
                    e = (dy - i) % NY
                    to, frm = (dy % 2) * GROUP, (e % 2) * GROUP
                    al[i, row + dy // 2 : row + dy // 2 + 1, to : to + GROUP] = st[i][
                        row + e // 2 : row + e // 2 + 1, frm : frm + GROUP
                    ]
        tops = [al[i, :PAIRS] for i in range(NY)]
        top = functools.reduce(jnp.maximum, tops)
        factors = [jnp.exp2(t - top) for t in tops]
        mass = sum(f * al[i, PAIRS : 2 * PAIRS] for i, f in enumerate(factors))
        share = sum(f * al[i, 2 * PAIRS :] for i, f in enumerate(factors))
        lse_s[...] = top + jnp.log2(mass)
        delta_s[...] = share / mass

        def one_pair(pair, _):
            low, high, t_low, t_high = row_limits(pair, xl, z, y, b)
            lse = lse_s[pl.ds(pair, 1), :]
            delta = delta_s[pl.ds(pair, 1), :]
            qp = qs[pair]
            up = us[pair]

            def tile(t, _):
                k = kc[pl.ds(2 * t, 2)].reshape(KT, HEAD)
                v = vc[pl.ds(2 * t, 2)].reshape(KT, HEAD)
                p = jnp.exp2(masked_scores(k, qp, t, low, high) - lse)
                ds = (p * (dot(v, up, NT) - delta)).astype(LOW)
                p = p.astype(LOW)
                dv[pl.ds(2 * t, 2)] += dot(p, up).reshape(2, CHUNK, HEAD)
                dk[pl.ds(2 * t, 2)] += dot(ds, qp).reshape(2, CHUNK, HEAD)
                kt_tile = jnp.concatenate([kt[2 * t], kt[2 * t + 1]], axis=1)
                dqt[pair] += dot(kt_tile, ds)
                return 0

            lax.fori_loop(t_low, t_high, tile, 0)
            return 0

        lax.fori_loop(0, PAIRS, one_pair, 0)

        for dy in range(NY):
            for o in range(2):
                for h in range(RATIO):
                    start = (dy % 2) * GROUP + h * CHUNK
                    part = dqt[o * 2 + dy // 2, :, start : start + CHUNK].T * SCALE
                    dq_out[dy][
                        o * CHUNK : (o + 1) * CHUNK, h * HEAD : (h + 1) * HEAD
                    ] = part.astype(dq_out[dy].dtype)
        for d in range(NZ):
            for o in range(2):
                at = key_chunk(xl, z, o, d)
                rows = slice(o * CHUNK, (o + 1) * CHUNK)
                dkv_out[d][rows, :HEAD] = (dk[at] * SCALE).astype(dkv_out[d].dtype)
                dkv_out[d][rows, HEAD:] = dv[at].astype(dkv_out[d].dtype)

    kept = (0, 2, NZ - 2)
    out = pl.pallas_call(
        kernel,
        in_specs=[sspec()] + [vspec()] * 28,
        out_specs=[vspec()] * 12,
        out_shape=[
            jax.ShapeDtypeStruct((2 * CHUNK, GROUP), WIDE if dy == 0 else LOW)
            for dy in range(NY)
        ]
        + [
            jax.ShapeDtypeStruct((2 * CHUNK, 2 * HEAD), WIDE if d in kept else LOW)
            for d in range(NZ)
        ],
        scratch_shapes=[
            pltpu.VMEM((PAIRS, ROWS, HEAD), LOW),
            pltpu.VMEM((PAIRS, ROWS, HEAD), LOW),
            pltpu.VMEM((XL * NZ, CHUNK, HEAD), LOW),
            pltpu.VMEM((XL * NZ, CHUNK, HEAD), LOW),
            pltpu.VMEM((XL * NZ, HEAD, CHUNK), LOW),
            pltpu.VMEM((XL * NZ, CHUNK, HEAD), WIDE),
            pltpu.VMEM((XL * NZ, CHUNK, HEAD), WIDE),
            pltpu.VMEM((PAIRS, HEAD, ROWS), WIDE),
            pltpu.VMEM((NY, 3 * PAIRS, ROWS), WIDE),
            pltpu.VMEM((PAIRS, ROWS), WIDE),
            pltpu.VMEM((PAIRS, ROWS), WIDE),
        ],
        compiler_params=params(),
        cost_estimate=pl.CostEstimate(
            flops=16 * 10**9, bytes_accessed=8 * 2**20, transcendentals=4 * 2**20
        ),
        name="backward",
    )(scalars, *stats, *q_blocks[0], *q_blocks[1], *u_blocks[0], *u_blocks[1], *kv_blocks)
    return out[:NY], out[NY:]


def shift(x, axis, size, d):
    return lax.ppermute(x, axis, [(i, (i - d) % size) for i in range(size)])


def per_device(queries, keys, values, grad_out, out_weight, segments):
    xl, z, y = lax.axis_index("xl"), lax.axis_index("z"), lax.axis_index("y")
    tp = lax.axis_index("xh") * 2 + lax.axis_index("core")

    def part(x, group, width):
        return lax.dynamic_slice_in_dim(x, group * width, width, 1)

    def key_value(group):
        return jnp.concatenate([part(keys, group, HEAD), part(values, group, HEAD)], axis=1)

    pos = jnp.stack([tp, xl]).astype(jnp.int32)
    far = shift(grad_out, "xh", 2, 1)
    mate = shift(grad_out, "core", 2, 1)
    kv_in = shift(key_value(1 - xl), "xl", 2, 1)
    q_in = shift(part(queries, 1 - xl, GROUP), "xl", 2, 1)
    q_own = part(queries, xl, GROUP)
    bound = lax.psum(jnp.sum((segments == 0).astype(jnp.int32)), ("xl", "z", "y"))
    scalars = jnp.stack([xl, z, y, bound]).astype(jnp.int32)

    kv_mine = jnp.concatenate([key_value(xl), kv_in], axis=0)
    kv_blocks = [kv_mine] + [None] * 7
    for d in (1, 7, 2, 6, 4):
        kv_blocks[d] = shift(kv_mine, "z", NZ, d)
    kv_blocks[3] = shift(kv_blocks[2], "z", NZ, 1)
    kv_blocks[5] = shift(kv_blocks[6], "z", NZ, -1)

    def along_y(x):
        return [x] + [shift(x, "y", NY, d) for d in (1, 2, 3)]

    q_blocks = [along_y(q_own), along_y(q_in)]

    u_part = up_first(pos, grad_out, mate, out_weight)
    far_mate = shift(far, "core", 2, 1)
    u_own, u_oth = up_second(pos, u_part, far, far_mate, out_weight)
    u_in = shift(u_oth, "xl", 2, 1)
    u_blocks = [along_y(u_own), along_y(u_in)]

    o_part, ml = forward(scalars, q_blocks, kv_blocks)
    mine = weighted(o_part, ml, u_blocks)
    stats = along_y(mine)
    dq, dkv = backward(scalars, stats, q_blocks, u_blocks, kv_blocks)

    up3 = shift(dkv[3], "z", NZ, -1)
    down3 = shift(dkv[5], "z", NZ, 1)
    got4 = shift(dkv[4], "z", NZ, 4)
    up2 = (dkv[2] + up3.astype(WIDE)).astype(LOW)
    down2 = (dkv[6] + down3.astype(WIDE)).astype(LOW)
    got = [
        shift(dkv[1], "z", NZ, -1),
        shift(dkv[7], "z", NZ, 1),
        shift(up2, "z", NZ, -2),
        shift(down2, "z", NZ, 2),
        got4,
    ]
    dkv_sum = dkv[0]
    for g in got:
        dkv_sum = dkv_sum + g.astype(WIDE)

    dq_sum = dq[0]
    for d in (1, 2, 3):
        dq_sum = dq_sum + shift(dq[d], "y", NY, -d).astype(WIDE)

    dq_back = shift(dq_sum[CHUNK:].astype(LOW), "xl", 2, 1)
    dkv_back = shift(dkv_sum[CHUNK:].astype(LOW), "xl", 2, 1)
    dq_own = dq_sum[:CHUNK].astype(LOW)
    dkv_own = dkv_sum[:CHUNK].astype(LOW)

    def join(a, c):
        return jnp.where(
            xl == 0, jnp.concatenate([a, c], axis=1), jnp.concatenate([c, a], axis=1)
        )

    return (
        join(dq_own, dq_back),
        join(dkv_own[:, :HEAD], dkv_back[:, :HEAD]),
        join(dkv_own[:, HEAD:], dkv_back[:, HEAD:]),
    )


def solution(mesh):
    fine = Mesh(mesh.devices.reshape(XL, NZ, NY, 2, 2), ("xl", "z", "y", "xh", "core"))
    ctx, tp = ("xl", "z", "y"), ("xh", "core")
    in_specs = (P(ctx, tp), P(ctx, tp), P(ctx, tp), P(ctx, tp), P(None, tp), P(ctx))
    out_specs = (P(ctx, tp), P(ctx, tp), P(ctx, tp))
    return jax.shard_map(
        per_device, mesh=fine, in_specs=in_specs, out_specs=out_specs, check_vma=False
    )
```

time: 1350 us -> 167 us (0.12)
  waiting for transfers between devices: 1060 us -> 17.8 us
  blocking collectives: 157 us -> 21.8 us
  starting transfers between devices: 0.2 us -> 90.3 us
  local copies, waits for them, and re-layouts: 66.5 us -> 6.42 us
  Pallas kernels: 0 us -> 28.2 us
  loops' own time: 22 us -> 0 us
  matrix products: 17.6 us -> 0 us
    reduce_scatter x2 -> x0, waiting for transfers between devices: 711 us -> none  [the longest x1 385 us: per_device(): lax.psum_scatter(value_terms, 'ctx', scatter_dimension=0, tiled=True)]
    all_gather x3 -> x0, waiting for transfers between devices: 349 us -> none  [the longest x1 244 us: per_device(): lax.all_gather(values, 'ctx', axis=0, tiled=True)]
    all_gather x1 -> x0, blocking collectives: 157 us -> none  [per_device(): lax.all_gather(segments, 'ctx', axis=0, tiled=True)]
    ppermute x0 -> x40, starting transfers between devices: none -> 90.3 us  [shift(): return lax.ppermute(x, axis, [(i, (i - d) % size) for i in range(size)])]
    pallas_call x0 -> x5, Pallas kernels: none -> 28.2 us  [the longest x1 12.8 us: backward(): pl.pallas_call(kernel, in_specs=[sspec()] + [vspec()] * 28, out_specs=[vs...]
    another operation x34 -> x0, loops' own time: 22 us -> none  [the longest x1 11.1 us: per_device(): lax.fori_loop(0, blocks, gradients, grad_state)]
    psum x0 -> x1, blocking collectives: none -> 21.8 us  [per_device(): lax.psum(jnp.sum((segments == 0).astype(jnp.int32)), ('xl', 'z', 'y'))]
    slice x32 -> x4, local copies, waits for them, and re-layouts: 19 us -> 0.04 us  [the longest x1 0.02 us: per_device(): dq_own = dq_sum[:CHUNK].astype(LOW)]
  transfers between devices with their start and end apart: 5 -> 40, of which waited for: 4 -> 10; matrix products, arithmetic and copies ran while one was open for 2% -> 3% of each run, Pallas kernels for 0% -> 9%
where the time goes in v1:
time: 167 us; the launch traced here: 169 us
  starting transfers between devices  90.3 us (54%)
  Pallas kernels  28.2 us (17%)
  blocking collectives  21.8 us (13%)
  waiting for transfers between devices  17.8 us (11%)
  local copies, waits for them, and re-layouts  6.42 us (4%)
  other arithmetic  3.82 us (2%)
    ppermute x40, starting transfers between devices, shift(): return lax.ppermute(x, axis, [(i, (i - d) % size) for i in range(size)])  90.3 us
    psum x1, blocking collectives, per_device(): lax.psum(jnp.sum((segments == 0).astype(jnp.int32)), ('xl', 'z', 'y'))  21.8 us
    ppermute x40, waiting for transfers between devices, shift(): return lax.ppermute(x, axis, [(i, (i - d) % size) for i in range(size)])  17.8 us
    pallas_call x1, Pallas kernels, backward(): pl.pallas_call(kernel, in_specs=[sspec()] + [vspec()] * 28, out_specs=[vs...  12.8 us
    pallas_call x1, Pallas kernels, forward(): pl.pallas_call(kernel, in_specs=[sspec()] + [vspec()] * 16, out_specs=[vs...  8.58 us
    unnamed x20, local copies, waits for them, and re-layouts  4.58 us
  transfers between devices with their start and end apart: 40, of which 10 were waited for; matrix products, arithmetic and copies ran while one was open for 3% of the time, Pallas kernels for 9%

profile of v1, /device:TPU:2, one launch (start us, length us, event | category | flops | bytes accessed | tf_op | source)
XLA Modules:
  0.0 169.2 jit_solution(16066820563914998160)
XLA Ops:
  0.6 2.2 %collective-permute-start.16 = (bf16[128,1024]{1,0:T(8,128)(2,1)}, bf16[128,1024]{1,0:T(8,128)(2,1)S(1)}, u32[]{:S(2)}, u32[]{:S(2)}) collective-permute-start(bf16[128,1024]{1,0:T(8,128)(2,1)} %g0.1), channel_id=1, source_target_pairs={{0,2},{2,0},{1,3},{3,1},{4,6},{6,4},{5,7},{7,5},{8,10},{10,8},{9,1... | collective-permute-start | bytes 786440 | tf_op jit(solution)/shard_map/ppermute | solution.py:358
  3.7 1.5 collective-permute-start.7
  5.2 1.0 constant_dynamic-slice_fusion.4
  6.9 1.6 collective-permute-start.2
  8.4 2.9 %collective-permute-start.1 = (bf16[128,512]{1,0:T(8,128)(2,1)S(1)}, bf16[128,512]{1,0:T(8,128)(2,1)S(1)}, u32[]{:S(2)}, u32[]{:S(2)}) collective-permute-start(bf16[128,512]{1,0:T(8,128)(2,1)S(1)} %get-tuple-element.38.refs_0_.refs_4_), channel_id=1, source_target_pairs={{0,8},{4,12},{8,0},{12,4},{1,9},{5,13},{9,1},{13,5},{2,10},{6,14},... | collective-permute-start | bytes 393224 | tf_op jit(solution)/shard_map/ppermute | solution.py:358
  11.3 1.7 %collective-permute-done.7 = bf16[128,256]{1,0:T(8,128)(2,1)S(1)} collective-permute-done((bf16[128,256]{1,0:T(8,128)(2,1)S(1)}, bf16[128,256]{1,0:T(8,128)(2,1)S(1)}, u32[]{:S(2)}, u32[]{:S(2)}) %collective-permute-start.7) | collective-permute-done | bytes 65568 | tf_op jit(solution)/shard_map/ppermute | solution.py:358
  13.6 1.1 collective-permute-done.3.refs_4_.refs_8_
  14.7 3.0 %collective-permute-start = (bf16[128,512]{1,0:T(8,128)(2,1)S(1)}, bf16[128,512]{1,0:T(8,128)(2,1)S(1)}, u32[]{:S(2)}, u32[]{:S(2)}) collective-permute-start(bf16[128,512]{1,0:T(8,128)(2,1)S(1)} %get-tuple-element.38.refs_0_.refs_4_), channel_id=1, source_target_pairs={{0,12},{4,0},{8,4},{12,8},{1,13},{5,1},{9,5},{13,9},{2,14},{6,2},{... | collective-permute-start | bytes 393224 | tf_op jit(solution)/shard_map/ppermute | solution.py:358
  17.7 1.9 %collective-permute-start.14 = (bf16[256,256]{1,0:T(8,128)(2,1)S(1)}, bf16[256,256]{1,0:T(8,128)(2,1)S(1)}, u32[]{:S(2)}, u32[]{:S(2)}) collective-permute-start(bf16[256,256]{1,0:T(8,128)(2,1)S(1)} %pad_maximum_fusion.refs_8_.refs_20_), channel_id=1, source_target_pairs={{0,16},{16,32},{32,48},{48,64},{64,80},{80,96},{96,112},{112,0},{1... | collective-permute-start | bytes 393224 | tf_op jit(solution)/shard_map/ppermute | solution.py:358
  19.7 3.3 %collective-permute-start.12 = (bf16[256,256]{1,0:T(8,128)(2,1)S(1)}, bf16[256,256]{1,0:T(8,128)(2,1)S(1)}, u32[]{:S(2)}, u32[]{:S(2)}) collective-permute-start(bf16[256,256]{1,0:T(8,128)(2,1)S(1)} %pad_maximum_fusion.refs_8_.refs_20_), channel_id=1, source_target_pairs={{0,32},{16,48},{32,64},{48,80},{64,96},{80,112},{96,0},{112,16},{1... | collective-permute-start | bytes 393224 | tf_op jit(solution)/shard_map/ppermute | solution.py:358
  22.9 4.5 %collective-permute-start.11 = (bf16[256,256]{1,0:T(8,128)(2,1)S(1)}, bf16[256,256]{1,0:T(8,128)(2,1)S(1)}, u32[]{:S(2)}, u32[]{:S(2)}) collective-permute-start(bf16[256,256]{1,0:T(8,128)(2,1)S(1)} %pad_maximum_fusion.refs_8_.refs_20_), channel_id=1, source_target_pairs={{0,64},{16,80},{32,96},{48,112},{64,0},{80,16},{96,32},{112,48},{1... | collective-permute-start | bytes 393224 | tf_op jit(solution)/shard_map/ppermute | solution.py:358
  27.4 1.2 collective-permute-done.14.refs_15_.refs_27_
  28.7 3.6 %collective-permute-start.9 = (bf16[256,256]{1,0:T(8,128)(2,1)S(1)}, bf16[256,256]{1,0:T(8,128)(2,1)S(1)}, u32[]{:S(2)}, u32[]{:S(2)}) collective-permute-start(bf16[256,256]{1,0:T(8,128)(2,1)S(1)} %pad_maximum_fusion.refs_8_.refs_20_), channel_id=1, source_target_pairs={{0,96},{16,112},{32,0},{48,16},{64,32},{80,48},{96,64},{112,80},{1... | collective-permute-start | bytes 393224 | tf_op jit(solution)/shard_map/ppermute | solution.py:358
  32.3 4.0 %collective-permute-done.12.refs_14_.refs_26_ = bf16[256,256]{1,0:T(8,128)(2,1)S(1)} collective-permute-done((bf16[256,256]{1,0:T(8,128)(2,1)S(1)}, bf16[256,256]{1,0:T(8,128)(2,1)S(1)}, u32[]{:S(2)}, u32[]{:S(2)}) %collective-permute-start.12) | collective-permute-done | bytes 131104 | tf_op jit(solution)/shard_map/ppermute | solution.py:358
  36.3 1.3 collective-permute-start.8
  37.6 1.6 collective-permute-start.5
  39.2 0.9 copy-done
  40.2 3.3 %upstream_first.1.part_ref = f32[128,1024]{1,0:T(8,128)S(1)} custom-call(s32[2]{0:T(128)S(1)} %pad_add_fusion.1.pos_ref, bf16[128,1024]{1,0:T(8,128)(2,1)S(1)} %copy-done, bf16[128,1024]{1,0:T(8,128)(2,1)S(1)} %collective-permute-done.15.g1, bf16[4096,1024]{1,0:T(8,128)(2,1)} %w_ref.3), custom_call_target="tpu_custom_call" | custom-call | tf_op jit(solution)/shard_map/upstream_first/pallas_call | solution.py:59
  43.5 3.3 %upstream_second.1 = (bf16[128,512]{1,0:T(8,128)(2,1)S(1)}, bf16[128,512]{1,0:T(8,128)(2,1)S(1)}) custom-call(s32[2]{0:T(128)S(1)} %pad_add_fusion.1.pos_ref, f32[128,1024]{1,0:T(8,128)S(1)} %upstream_first.1.part_ref, bf16[128,1024]{1,0:T(8,128)(2,1)S(1)} %collective-permute-done.16.g0, bf16[128,1024]{1,0:T(8,128)(2,1)S(1)} %collective-permute-done.17.g1, ...), custom_call_target="tpu_custom_call" | custom-call | tf_op jit(solution)/shard_map/upstream_second/pallas_call | solution.py:92
  46.8 1.8 %collective-permute-start.4 = (bf16[128,512]{1,0:T(8,128)(2,1)S(1)}, bf16[128,512]{1,0:T(8,128)(2,1)S(1)}, u32[]{:S(2)}, u32[]{:S(2)}) collective-permute-start(bf16[128,512]{1,0:T(8,128)(2,1)S(1)} %collective-permute-done.3.refs_4_.refs_8_), channel_id=1, source_target_pairs={{0,12},{4,0},{8,4},{12,8},{1,13},{5,1},{9,5},{13,9},{2,14},{6,2},{... | collective-permute-start | bytes 393224 | tf_op jit(solution)/shard_map/ppermute | solution.py:358
  48.5 1.4 collective-permute-start.13
  49.9 1.8 %collective-permute-start.10 = (bf16[256,256]{1,0:T(8,128)(2,1)S(1)}, bf16[256,256]{1,0:T(8,128)(2,1)S(1)}, u32[]{:S(2)}, u32[]{:S(2)}) collective-permute-start(bf16[256,256]{1,0:T(8,128)(2,1)S(1)} %collective-permute-done.9.refs_10_.refs_22_), channel_id=1, source_target_pairs={{0,112},{16,0},{32,16},{48,32},{64,48},{80,64},{96,80},{112,96},{1... | collective-permute-start | bytes 393224 | tf_op jit(solution)/shard_map/ppermute | solution.py:358
  52.4 1.1 collective-permute-start.20
  54.1 21.8 %psum.7 = s32[1]{0:T(128)} all-reduce(s32[1]{0:T(128)} %bitcast.3), channel_id=1, replica_groups=mesh['xl'=2,'z'=8,'y'=4,'xh'=2,'core'=2] {'xl','z','y'}, use_global_device_ids=true, to_apply=%region_1.0 | all-reduce | flops 1 | bytes 8 | tf_op jit(solution)/shard_map/psum | solution.py:377
  76.6 1.8 %collective-permute-start.19 = (bf16[128,512]{1,0:T(8,128)(2,1)S(1)}, bf16[128,512]{1,0:T(8,128)(2,1)S(1)}, u32[]{:S(2)}, u32[]{:S(2)}) collective-permute-start(bf16[128,512]{1,0:T(8,128)(2,1)S(1)} %get-tuple-element.21.refs_0_.refs_12_), channel_id=1, source_target_pairs={{0,8},{4,12},{8,0},{12,4},{1,9},{5,13},{9,1},{13,5},{2,10},{6,14},... | collective-permute-start | bytes 393224 | tf_op jit(solution)/shard_map/ppermute | solution.py:358
  78.4 2.1 %collective-permute-start.18 = (bf16[128,512]{1,0:T(8,128)(2,1)S(1)}, bf16[128,512]{1,0:T(8,128)(2,1)S(1)}, u32[]{:S(2)}, u32[]{:S(2)}) collective-permute-start(bf16[128,512]{1,0:T(8,128)(2,1)S(1)} %get-tuple-element.21.refs_0_.refs_12_), channel_id=1, source_target_pairs={{0,12},{4,0},{8,4},{12,8},{1,13},{5,1},{9,5},{13,9},{2,14},{6,2},{... | collective-permute-start | bytes 393224 | tf_op jit(solution)/shard_map/ppermute | solution.py:358
  80.6 1.8 %collective-permute-start.23 = (bf16[128,512]{1,0:T(8,128)(2,1)S(1)}, bf16[128,512]{1,0:T(8,128)(2,1)S(1)}, u32[]{:S(2)}, u32[]{:S(2)}) collective-permute-start(bf16[128,512]{1,0:T(8,128)(2,1)S(1)} %collective-permute-done.21.refs_4_.refs_16_), channel_id=1, source_target_pairs={{0,8},{4,12},{8,0},{12,4},{1,9},{5,13},{9,1},{13,5},{2,10},{6,14},... | collective-permute-start | bytes 393224 | tf_op jit(solution)/shard_map/ppermute | solution.py:358
  82.4 2.5 %collective-permute-start.22 = (bf16[128,512]{1,0:T(8,128)(2,1)S(1)}, bf16[128,512]{1,0:T(8,128)(2,1)S(1)}, u32[]{:S(2)}, u32[]{:S(2)}) collective-permute-start(bf16[128,512]{1,0:T(8,128)(2,1)S(1)} %collective-permute-done.21.refs_4_.refs_16_), channel_id=1, source_target_pairs={{0,12},{4,0},{8,4},{12,8},{1,13},{5,1},{9,5},{13,9},{2,14},{6,2},{... | collective-permute-start | bytes 393224 | tf_op jit(solution)/shard_map/ppermute | solution.py:358
  84.9 8.6 %forward.1 = (f32[4,144,1024]{2,1,0:T(8,128)S(1)}, f32[8,1024]{1,0:T(8,128)S(1)}) custom-call(s32[4]{0:T(128)S(1)} %pad_add_fusion.sc, bf16[128,512]{1,0:T(8,128)(2,1)S(1)} %get-tuple-element.38.refs_0_.refs_4_, bf16[128,512]{1,0:T(8,128)(2,1)S(1)} %collective-permute-done.refs_1_.refs_5_, bf16[128,512]{1,0:T(8,128)(2,1)S(1)} %collective-permute-done.1.refs_2_.refs_6_, ...), custom_call_target="tpu_custom_call" | custom-call | flops 8000000000 | bytes 6291456 | tf_op jit(solution)/shard_map/forward/pallas_call | solution.py:196
  94.0 1.3 collective-permute-start.27
  96.0 2.5 %collective-permute-start.25 = (f32[12,1024]{1,0:T(8,128)S(1)}, f32[12,1024]{1,0:T(8,128)S(1)}, u32[]{:S(2)}, u32[]{:S(2)}) collective-permute-start(f32[12,1024]{1,0:T(8,128)S(1)} %weighted.1.refs_0_), channel_id=1, source_target_pairs={{0,12},{4,0},{8,4},{12,8},{1,13},{5,1},{9,5},{13,9},{2,14},{6,2},{... | collective-permute-start | bytes 147464 | tf_op jit(solution)/shard_map/ppermute | solution.py:358
  98.5 1.0 collective-permute-done.27.refs_3_
  99.5 1.5 collective-permute-done.26.refs_2_
  101.1 0.9 copy-done.2
  102.0 0.9 copy-done.4
  103.8 0.9 copy-done.8
  104.7 12.8 %backward.1 = (f32[256,512]{1,0:T(8,128)S(1)}, bf16[256,512]{1,0:T(8,128)(2,1)S(1)}, bf16[256,512]{1,0:T(8,128)(2,1)S(1)}, bf16[256,512]{1,0:T(8,128)(2,1)S(1)},...) custom-call(s32[4]{0:T(128)S(1)} %pad_add_fusion.sc, ...), custom_call_target="tpu_custom_call" | custom-call | flops 16000000000 | bytes 8388608 | tf_op jit(solution)/shard_map/backward/pallas_call | solution.py:323
  117.4 1.8 %collective-permute-start.34 = (bf16[256,256]{1,0:T(8,128)(2,1)S(1)}, bf16[256,256]{1,0:T(8,128)(2,1)S(1)}, u32[]{:S(2)}, u32[]{:S(2)}) collective-permute-start(bf16[256,256]{1,0:T(8,128)(2,1)S(1)} %get-tuple-element.31), channel_id=1, source_target_pairs={{0,16},{16,32},{32,48},{48,64},{64,80},{80,96},{96,112},{112,0},{1... | collective-permute-start | bytes 393224 | tf_op jit(solution)/shard_map/ppermute | solution.py:358
  119.2 5.1 %collective-permute-start.32 = (bf16[256,256]{1,0:T(8,128)(2,1)}, bf16[256,256]{1,0:T(8,128)(2,1)S(1)}, u32[]{:S(2)}, u32[]{:S(2)}) collective-permute-start(bf16[256,256]{1,0:T(8,128)(2,1)} %get-tuple-element.28), channel_id=1, source_target_pairs={{0,16},{16,32},{32,48},{48,64},{64,80},{80,96},{96,112},{112,0},{1... | collective-permute-start | bytes 393224 | tf_op jit(solution)/shard_map/ppermute | solution.py:358
  124.3 13.8 %collective-permute-start.33 = (bf16[256,256]{1,0:T(8,128)(2,1)}, bf16[256,256]{1,0:T(8,128)(2,1)S(1)}, u32[]{:S(2)}, u32[]{:S(2)}) collective-permute-start(bf16[256,256]{1,0:T(8,128)(2,1)} %get-tuple-element.29), channel_id=1, source_target_pairs={{0,112},{16,0},{32,16},{48,32},{64,48},{80,64},{96,80},{112,96},{1... | collective-permute-start | bytes 393224 | tf_op jit(solution)/shard_map/ppermute | solution.py:358
  138.1 2.0 %collective-permute-start.36 = (bf16[256,256]{1,0:T(8,128)(2,1)S(1)}, bf16[256,256]{1,0:T(8,128)(2,1)S(1)}, u32[]{:S(2)}, u32[]{:S(2)}) collective-permute-start(bf16[256,256]{1,0:T(8,128)(2,1)S(1)} %get-tuple-element.33), channel_id=1, source_target_pairs={{0,112},{16,0},{32,16},{48,32},{64,48},{80,64},{96,80},{112,96},{1... | collective-permute-start | bytes 393224 | tf_op jit(solution)/shard_map/ppermute | solution.py:358
  141.0 3.0 %collective-permute-start.35 = (bf16[256,256]{1,0:T(8,128)(2,1)S(1)}, bf16[256,256]{1,0:T(8,128)(2,1)S(1)}, u32[]{:S(2)}, u32[]{:S(2)}) collective-permute-start(bf16[256,256]{1,0:T(8,128)(2,1)S(1)} %add_convert_fusion.3), channel_id=1, source_target_pairs={{0,32},{16,48},{32,64},{48,80},{64,96},{80,112},{96,0},{112,16},{1... | collective-permute-start | bytes 393224 | tf_op jit(solution)/shard_map/ppermute | solution.py:358
  144.0 2.5 %collective-permute-start.37 = (bf16[256,256]{1,0:T(8,128)(2,1)S(1)}, bf16[256,256]{1,0:T(8,128)(2,1)S(1)}, u32[]{:S(2)}, u32[]{:S(2)}) collective-permute-start(bf16[256,256]{1,0:T(8,128)(2,1)S(1)} %add_convert_fusion.2), channel_id=1, source_target_pairs={{0,96},{16,112},{32,0},{48,16},{64,32},{80,48},{96,64},{112,80},{1... | collective-permute-start | bytes 393224 | tf_op jit(solution)/shard_map/ppermute | solution.py:358
  146.6 5.1 %collective-permute-start.28 = (bf16[256,512]{1,0:T(8,128)(2,1)S(1)}, bf16[256,512]{1,0:T(8,128)(2,1)S(1)}, u32[]{:S(2)}, u32[]{:S(2)}) collective-permute-start(bf16[256,512]{1,0:T(8,128)(2,1)S(1)} %get-tuple-element.24), channel_id=1, source_target_pairs={{0,4},{4,8},{8,12},{12,0},{1,5},{5,9},{9,13},{13,1},{2,6},{6,10},{... | collective-permute-start | bytes 786440 | tf_op jit(solution)/shard_map/ppermute | solution.py:358
  151.6 3.8 %collective-permute-start.29 = (bf16[256,512]{1,0:T(8,128)(2,1)S(1)}, bf16[256,512]{1,0:T(8,128)(2,1)S(1)}, u32[]{:S(2)}, u32[]{:S(2)}) collective-permute-start(bf16[256,512]{1,0:T(8,128)(2,1)S(1)} %get-tuple-element.25), channel_id=1, source_target_pairs={{0,8},{4,12},{8,0},{12,4},{1,9},{5,13},{9,1},{13,5},{2,10},{6,14},... | collective-permute-start | bytes 786440 | tf_op jit(solution)/shard_map/ppermute | solution.py:358
  155.5 3.8 %collective-permute-start.30 = (bf16[256,512]{1,0:T(8,128)(2,1)S(1)}, bf16[256,512]{1,0:T(8,128)(2,1)S(1)}, u32[]{:S(2)}, u32[]{:S(2)}) collective-permute-start(bf16[256,512]{1,0:T(8,128)(2,1)S(1)} %get-tuple-element.26), channel_id=1, source_target_pairs={{0,12},{4,0},{8,4},{12,8},{1,13},{5,1},{9,5},{13,9},{2,14},{6,2},{... | collective-permute-start | bytes 786440 | tf_op jit(solution)/shard_map/ppermute | solution.py:358
  160.1 2.5 %collective-permute-done.29 = bf16[256,512]{1,0:T(8,128)(2,1)S(1)} collective-permute-done((bf16[256,512]{1,0:T(8,128)(2,1)S(1)}, bf16[256,512]{1,0:T(8,128)(2,1)S(1)}, u32[]{:S(2)}, u32[]{:S(2)}) %collective-permute-start.29) | collective-permute-done | bytes 262176 | tf_op jit(solution)/shard_map/ppermute | solution.py:358
  165.3 3.1 %collective-permute-done.31 = bf16[128,512]{1,0:T(8,128)(2,1)S(1)} collective-permute-done((bf16[128,512]{1,0:T(8,128)(2,1)S(1)}, bf16[128,512]{1,0:T(8,128)(2,1)S(1)}, u32[]{:S(2)}, u32[]{:S(2)}) %collective-permute-start.31) | collective-permute-done | bytes 131104 | tf_op jit(solution)/shard_map/ppermute | solution.py:358
  (76 shorter events, 11.4 us)
Async XLA Ops:
  0.6 12.4 %collective-permute-start.16 = (bf16[128,1024]{1,0:T(8,128)(2,1)}, bf16[128,1024]{1,0:T(8,128)(2,1)S(1)}, u32[]{:S(2)}, u32[]{:S(2)}) collective-permute-start(bf16[128,1024]{1,0:T(8,128)(2,1)} %g0.1), channel_id=1, source_target_pairs={{0,2},{2,0},{1,3},{3,1},{4,6},{6,4},{5,7},{7,5},{8,10},{10,8},{9,1... | collective-permute-start | bytes 786440 | tf_op jit(solution)/shard_map/ppermute | solution.py:358
  3.7 9.4 %collective-permute-start.7 = (bf16[128,256]{1,0:T(8,128)(2,1)S(1)}, bf16[128,256]{1,0:T(8,128)(2,1)S(1)}, u32[]{:S(2)}, u32[]{:S(2)}) collective-permute-start(bf16[128,256]{1,0:T(8,128)(2,1)S(1)} %pad_maximum_fusion.1), channel_id=1, source_target_pairs={{0,128},{128,0},{1,129},{129,1},{2,130},{130,2},{3,131},{131,3},{4... | collective-permute-start | bytes 196616 | tf_op jit(solution)/shard_map/ppermute | solution.py:358
  6.2 8.5 %collective-permute-start.3 = (bf16[128,512]{1,0:T(8,128)(2,1)S(1)}, bf16[128,512]{1,0:T(8,128)(2,1)S(1)}, u32[]{:S(2)}, u32[]{:S(2)}) collective-permute-start(bf16[128,512]{1,0:T(8,128)(2,1)S(1)} %get-tuple-element.37), channel_id=1, source_target_pairs={{0,128},{128,0},{1,129},{129,1},{2,130},{130,2},{3,131},{131,3},{4... | collective-permute-start | bytes 393224 | tf_op jit(solution)/shard_map/ppermute | solution.py:358
  6.9 10.9 %collective-permute-start.2 = (bf16[128,512]{1,0:T(8,128)(2,1)S(1)}, bf16[128,512]{1,0:T(8,128)(2,1)S(1)}, u32[]{:S(2)}, u32[]{:S(2)}) collective-permute-start(bf16[128,512]{1,0:T(8,128)(2,1)S(1)} %get-tuple-element.38.refs_0_.refs_4_), channel_id=1, source_target_pairs={{0,4},{4,8},{8,12},{12,0},{1,5},{5,9},{9,13},{13,1},{2,6},{6,10},{... | collective-permute-start | bytes 393224 | tf_op jit(solution)/shard_map/ppermute | solution.py:358
  8.4 11.2 %collective-permute-start.1 = (bf16[128,512]{1,0:T(8,128)(2,1)S(1)}, bf16[128,512]{1,0:T(8,128)(2,1)S(1)}, u32[]{:S(2)}, u32[]{:S(2)}) collective-permute-start(bf16[128,512]{1,0:T(8,128)(2,1)S(1)} %get-tuple-element.38.refs_0_.refs_4_), channel_id=1, source_target_pairs={{0,8},{4,12},{8,0},{12,4},{1,9},{5,13},{9,1},{13,5},{2,10},{6,14},... | collective-permute-start | bytes 393224 | tf_op jit(solution)/shard_map/ppermute | solution.py:358
  13.1 24.5 %collective-permute-start.15 = (bf16[128,1024]{1,0:T(8,128)(2,1)}, bf16[128,1024]{1,0:T(8,128)(2,1)S(1)}, u32[]{:S(2)}, u32[]{:S(2)}) collective-permute-start(bf16[128,1024]{1,0:T(8,128)(2,1)} %g0.1), channel_id=1, source_target_pairs={{0,1},{1,0},{2,3},{3,2},{4,5},{5,4},{6,7},{7,6},{8,9},{9,8},{10,11... | collective-permute-start | bytes 786440 | tf_op jit(solution)/shard_map/ppermute | solution.py:358
  13.1 24.5 %collective-permute-start.17 = (bf16[128,1024]{1,0:T(8,128)(2,1)S(1)}, bf16[128,1024]{1,0:T(8,128)(2,1)S(1)}, u32[]{:S(2)}, u32[]{:S(2)}) collective-permute-start(bf16[128,1024]{1,0:T(8,128)(2,1)S(1)} %collective-permute-done.16.g0), channel_id=1, source_target_pairs={{0,1},{1,0},{2,3},{3,2},{4,5},{5,4},{6,7},{7,6},{8,9},{9,8},{10,11... | collective-permute-start | bytes 786440 | tf_op jit(solution)/shard_map/ppermute | solution.py:358
  14.7 8.2 %collective-permute-start = (bf16[128,512]{1,0:T(8,128)(2,1)S(1)}, bf16[128,512]{1,0:T(8,128)(2,1)S(1)}, u32[]{:S(2)}, u32[]{:S(2)}) collective-permute-start(bf16[128,512]{1,0:T(8,128)(2,1)S(1)} %get-tuple-element.38.refs_0_.refs_4_), channel_id=1, source_target_pairs={{0,12},{4,0},{8,4},{12,8},{1,13},{5,1},{9,5},{13,9},{2,14},{6,2},{... | collective-permute-start | bytes 393224 | tf_op jit(solution)/shard_map/ppermute | solution.py:358
  17.7 10.9 %collective-permute-start.14 = (bf16[256,256]{1,0:T(8,128)(2,1)S(1)}, bf16[256,256]{1,0:T(8,128)(2,1)S(1)}, u32[]{:S(2)}, u32[]{:S(2)}) collective-permute-start(bf16[256,256]{1,0:T(8,128)(2,1)S(1)} %pad_maximum_fusion.refs_8_.refs_20_), channel_id=1, source_target_pairs={{0,16},{16,32},{32,48},{48,64},{64,80},{80,96},{96,112},{112,0},{1... | collective-permute-start | bytes 393224 | tf_op jit(solution)/shard_map/ppermute | solution.py:358
  19.7 16.7 %collective-permute-start.12 = (bf16[256,256]{1,0:T(8,128)(2,1)S(1)}, bf16[256,256]{1,0:T(8,128)(2,1)S(1)}, u32[]{:S(2)}, u32[]{:S(2)}) collective-permute-start(bf16[256,256]{1,0:T(8,128)(2,1)S(1)} %pad_maximum_fusion.refs_8_.refs_20_), channel_id=1, source_target_pairs={{0,32},{16,48},{32,64},{48,80},{64,96},{80,112},{96,0},{112,16},{1... | collective-permute-start | bytes 393224 | tf_op jit(solution)/shard_map/ppermute | solution.py:358
  22.9 23.8 %collective-permute-start.11 = (bf16[256,256]{1,0:T(8,128)(2,1)S(1)}, bf16[256,256]{1,0:T(8,128)(2,1)S(1)}, u32[]{:S(2)}, u32[]{:S(2)}) collective-permute-start(bf16[256,256]{1,0:T(8,128)(2,1)S(1)} %pad_maximum_fusion.refs_8_.refs_20_), channel_id=1, source_target_pairs={{0,64},{16,80},{32,96},{48,112},{64,0},{80,16},{96,32},{112,48},{1... | collective-permute-start | bytes 393224 | tf_op jit(solution)/shard_map/ppermute | solution.py:358
  28.7 19.8 %collective-permute-start.9 = (bf16[256,256]{1,0:T(8,128)(2,1)S(1)}, bf16[256,256]{1,0:T(8,128)(2,1)S(1)}, u32[]{:S(2)}, u32[]{:S(2)}) collective-permute-start(bf16[256,256]{1,0:T(8,128)(2,1)S(1)} %pad_maximum_fusion.refs_8_.refs_20_), channel_id=1, source_target_pairs={{0,96},{16,112},{32,0},{48,16},{64,32},{80,48},{96,64},{112,80},{1... | collective-permute-start | bytes 393224 | tf_op jit(solution)/shard_map/ppermute | solution.py:358
  36.3 13.6 %collective-permute-start.8 = (bf16[256,256]{1,0:T(8,128)(2,1)S(1)}, bf16[256,256]{1,0:T(8,128)(2,1)S(1)}, u32[]{:S(2)}, u32[]{:S(2)}) collective-permute-start(bf16[256,256]{1,0:T(8,128)(2,1)S(1)} %pad_maximum_fusion.refs_8_.refs_20_), channel_id=1, source_target_pairs={{0,112},{16,0},{32,16},{48,32},{64,48},{80,64},{96,80},{112,96},{1... | collective-permute-start | bytes 393224 | tf_op jit(solution)/shard_map/ppermute | solution.py:358
  37.6 14.2 %collective-permute-start.6 = (bf16[128,512]{1,0:T(8,128)(2,1)S(1)}, bf16[128,512]{1,0:T(8,128)(2,1)S(1)}, u32[]{:S(2)}, u32[]{:S(2)}) collective-permute-start(bf16[128,512]{1,0:T(8,128)(2,1)S(1)} %collective-permute-done.3.refs_4_.refs_8_), channel_id=1, source_target_pairs={{0,4},{4,8},{8,12},{12,0},{1,5},{5,9},{9,13},{13,1},{2,6},{6,10},{... | collective-permute-start | bytes 393224 | tf_op jit(solution)/shard_map/ppermute | solution.py:358
  37.6 14.7 %collective-permute-start.5 = (bf16[128,512]{1,0:T(8,128)(2,1)S(1)}, bf16[128,512]{1,0:T(8,128)(2,1)S(1)}, u32[]{:S(2)}, u32[]{:S(2)}) collective-permute-start(bf16[128,512]{1,0:T(8,128)(2,1)S(1)} %collective-permute-done.3.refs_4_.refs_8_), channel_id=1, source_target_pairs={{0,8},{4,12},{8,0},{12,4},{1,9},{5,13},{9,1},{13,5},{2,10},{6,14},... | collective-permute-start | bytes 393224 | tf_op jit(solution)/shard_map/ppermute | solution.py:358
  39.2 0.9 copy-start
  40.2 13.3 %copy-start.9 = (s32[128]{0:T(128)S(1)}, s32[128]{0:T(128)}, u32[]{:S(2)}) copy-start(s32[128]{0:T(128)} %param.11) | copy-start | bytes 1540
  46.8 29.9 %collective-permute-start.4 = (bf16[128,512]{1,0:T(8,128)(2,1)S(1)}, bf16[128,512]{1,0:T(8,128)(2,1)S(1)}, u32[]{:S(2)}, u32[]{:S(2)}) collective-permute-start(bf16[128,512]{1,0:T(8,128)(2,1)S(1)} %collective-permute-done.3.refs_4_.refs_8_), channel_id=1, source_target_pairs={{0,12},{4,0},{8,4},{12,8},{1,13},{5,1},{9,5},{13,9},{2,14},{6,2},{... | collective-permute-start | bytes 393224 | tf_op jit(solution)/shard_map/ppermute | solution.py:358
  48.5 29.9 %collective-permute-start.13 = (bf16[256,256]{1,0:T(8,128)(2,1)S(1)}, bf16[256,256]{1,0:T(8,128)(2,1)S(1)}, u32[]{:S(2)}, u32[]{:S(2)}) collective-permute-start(bf16[256,256]{1,0:T(8,128)(2,1)S(1)} %collective-permute-done.12.refs_14_.refs_26_), channel_id=1, source_target_pairs={{0,16},{16,32},{32,48},{48,64},{64,80},{80,96},{96,112},{112,0},{1... | collective-permute-start | bytes 393224 | tf_op jit(solution)/shard_map/ppermute | solution.py:358
  49.9 30.7 %collective-permute-start.10 = (bf16[256,256]{1,0:T(8,128)(2,1)S(1)}, bf16[256,256]{1,0:T(8,128)(2,1)S(1)}, u32[]{:S(2)}, u32[]{:S(2)}) collective-permute-start(bf16[256,256]{1,0:T(8,128)(2,1)S(1)} %collective-permute-done.9.refs_10_.refs_22_), channel_id=1, source_target_pairs={{0,112},{16,0},{32,16},{48,32},{64,48},{80,64},{96,80},{112,96},{1... | collective-permute-start | bytes 393224 | tf_op jit(solution)/shard_map/ppermute | solution.py:358
  51.8 28.8 %collective-permute-start.21 = (bf16[128,512]{1,0:T(8,128)(2,1)S(1)}, bf16[128,512]{1,0:T(8,128)(2,1)S(1)}, u32[]{:S(2)}, u32[]{:S(2)}) collective-permute-start(bf16[128,512]{1,0:T(8,128)(2,1)S(1)} %get-tuple-element.22), channel_id=1, source_target_pairs={{0,128},{128,0},{1,129},{129,1},{2,130},{130,2},{3,131},{131,3},{4... | collective-permute-start | bytes 393224 | tf_op jit(solution)/shard_map/ppermute | solution.py:358
  52.4 41.1 %copy-start.1 = (bf16[128,512]{1,0:T(8,128)(2,1)}, bf16[128,512]{1,0:T(8,128)(2,1)S(1)}, u32[]{:S(2)}) copy-start(bf16[128,512]{1,0:T(8,128)(2,1)S(1)} %collective-permute-done.5.refs_6_.refs_10_) | copy-start | bytes 393220
  52.4 30.0 %collective-permute-start.20 = (bf16[128,512]{1,0:T(8,128)(2,1)S(1)}, bf16[128,512]{1,0:T(8,128)(2,1)S(1)}, u32[]{:S(2)}, u32[]{:S(2)}) collective-permute-start(bf16[128,512]{1,0:T(8,128)(2,1)S(1)} %get-tuple-element.21.refs_0_.refs_12_), channel_id=1, source_target_pairs={{0,4},{4,8},{8,12},{12,0},{1,5},{5,9},{9,13},{13,1},{2,6},{6,10},{... | collective-permute-start | bytes 393224 | tf_op jit(solution)/shard_map/ppermute | solution.py:358
  76.6 16.9 %copy-start.3 = (bf16[128,512]{1,0:T(8,128)(2,1)}, bf16[128,512]{1,0:T(8,128)(2,1)S(1)}, u32[]{:S(2)}) copy-start(bf16[128,512]{1,0:T(8,128)(2,1)S(1)} %collective-permute-done.4.refs_5_.refs_9_) | copy-start | bytes 393220
  76.6 16.9 %collective-permute-start.19 = (bf16[128,512]{1,0:T(8,128)(2,1)S(1)}, bf16[128,512]{1,0:T(8,128)(2,1)S(1)}, u32[]{:S(2)}, u32[]{:S(2)}) collective-permute-start(bf16[128,512]{1,0:T(8,128)(2,1)S(1)} %get-tuple-element.21.refs_0_.refs_12_), channel_id=1, source_target_pairs={{0,8},{4,12},{8,0},{12,4},{1,9},{5,13},{9,1},{13,5},{2,10},{6,14},... | collective-permute-start | bytes 393224 | tf_op jit(solution)/shard_map/ppermute | solution.py:358
  78.4 15.1 %copy-start.5 = (bf16[256,256]{1,0:T(8,128)(2,1)}, bf16[256,256]{1,0:T(8,128)(2,1)S(1)}, u32[]{:S(2)}) copy-start(bf16[256,256]{1,0:T(8,128)(2,1)S(1)} %collective-permute-done.13.refs_13_.refs_25_) | copy-start | bytes 393220
  78.4 15.1 %collective-permute-start.18 = (bf16[128,512]{1,0:T(8,128)(2,1)S(1)}, bf16[128,512]{1,0:T(8,128)(2,1)S(1)}, u32[]{:S(2)}, u32[]{:S(2)}) collective-permute-start(bf16[128,512]{1,0:T(8,128)(2,1)S(1)} %get-tuple-element.21.refs_0_.refs_12_), channel_id=1, source_target_pairs={{0,12},{4,0},{8,4},{12,8},{1,13},{5,1},{9,5},{13,9},{2,14},{6,2},{... | collective-permute-start | bytes 393224 | tf_op jit(solution)/shard_map/ppermute | solution.py:358
  80.6 13.0 %collective-permute-start.24 = (bf16[128,512]{1,0:T(8,128)(2,1)S(1)}, bf16[128,512]{1,0:T(8,128)(2,1)S(1)}, u32[]{:S(2)}, u32[]{:S(2)}) collective-permute-start(bf16[128,512]{1,0:T(8,128)(2,1)S(1)} %collective-permute-done.21.refs_4_.refs_16_), channel_id=1, source_target_pairs={{0,4},{4,8},{8,12},{12,0},{1,5},{5,9},{9,13},{13,1},{2,6},{6,10},{... | collective-permute-start | bytes 393224 | tf_op jit(solution)/shard_map/ppermute | solution.py:358
  80.6 12.9 %copy-start.7 = (bf16[256,256]{1,0:T(8,128)(2,1)}, bf16[256,256]{1,0:T(8,128)(2,1)S(1)}, u32[]{:S(2)}) copy-start(bf16[256,256]{1,0:T(8,128)(2,1)S(1)} %collective-permute-done.10.refs_11_.refs_23_) | copy-start | bytes 393220
  80.6 13.0 %collective-permute-start.23 = (bf16[128,512]{1,0:T(8,128)(2,1)S(1)}, bf16[128,512]{1,0:T(8,128)(2,1)S(1)}, u32[]{:S(2)}, u32[]{:S(2)}) collective-permute-start(bf16[128,512]{1,0:T(8,128)(2,1)S(1)} %collective-permute-done.21.refs_4_.refs_16_), channel_id=1, source_target_pairs={{0,8},{4,12},{8,0},{12,4},{1,9},{5,13},{9,1},{13,5},{2,10},{6,14},... | collective-permute-start | bytes 393224 | tf_op jit(solution)/shard_map/ppermute | solution.py:358
  82.4 11.2 %collective-permute-start.22 = (bf16[128,512]{1,0:T(8,128)(2,1)S(1)}, bf16[128,512]{1,0:T(8,128)(2,1)S(1)}, u32[]{:S(2)}, u32[]{:S(2)}) collective-permute-start(bf16[128,512]{1,0:T(8,128)(2,1)S(1)} %collective-permute-done.21.refs_4_.refs_16_), channel_id=1, source_target_pairs={{0,12},{4,0},{8,4},{12,8},{1,13},{5,1},{9,5},{13,9},{2,14},{6,2},{... | collective-permute-start | bytes 393224 | tf_op jit(solution)/shard_map/ppermute | solution.py:358
  94.0 5.6 %collective-permute-start.27 = (f32[12,1024]{1,0:T(8,128)S(1)}, f32[12,1024]{1,0:T(8,128)S(1)}, u32[]{:S(2)}, u32[]{:S(2)}) collective-permute-start(f32[12,1024]{1,0:T(8,128)S(1)} %weighted.1.refs_0_), channel_id=1, source_target_pairs={{0,4},{4,8},{8,12},{12,0},{1,5},{5,9},{9,13},{13,1},{2,6},{6,10},{... | collective-permute-start | bytes 147464 | tf_op jit(solution)/shard_map/ppermute | solution.py:358
  95.3 5.8 %collective-permute-start.26 = (f32[12,1024]{1,0:T(8,128)S(1)}, f32[12,1024]{1,0:T(8,128)S(1)}, u32[]{:S(2)}, u32[]{:S(2)}) collective-permute-start(f32[12,1024]{1,0:T(8,128)S(1)} %weighted.1.refs_0_), channel_id=1, source_target_pairs={{0,8},{4,12},{8,0},{12,4},{1,9},{5,13},{9,1},{13,5},{2,10},{6,14},... | collective-permute-start | bytes 147464 | tf_op jit(solution)/shard_map/ppermute | solution.py:358
  96.0 5.1 %collective-permute-start.25 = (f32[12,1024]{1,0:T(8,128)S(1)}, f32[12,1024]{1,0:T(8,128)S(1)}, u32[]{:S(2)}, u32[]{:S(2)}) collective-permute-start(f32[12,1024]{1,0:T(8,128)S(1)} %weighted.1.refs_0_), channel_id=1, source_target_pairs={{0,12},{4,0},{8,4},{12,8},{1,13},{5,1},{9,5},{13,9},{2,14},{6,2},{... | collective-permute-start | bytes 147464 | tf_op jit(solution)/shard_map/ppermute | solution.py:358
  101.1 0.9 copy-start.2
  102.0 0.9 copy-start.4
  117.4 23.5 %collective-permute-start.34 = (bf16[256,256]{1,0:T(8,128)(2,1)S(1)}, bf16[256,256]{1,0:T(8,128)(2,1)S(1)}, u32[]{:S(2)}, u32[]{:S(2)}) collective-permute-start(bf16[256,256]{1,0:T(8,128)(2,1)S(1)} %get-tuple-element.31), channel_id=1, source_target_pairs={{0,16},{16,32},{32,48},{48,64},{64,80},{80,96},{96,112},{112,0},{1... | collective-permute-start | bytes 393224 | tf_op jit(solution)/shard_map/ppermute | solution.py:358
  119.2 27.3 %collective-permute-start.32 = (bf16[256,256]{1,0:T(8,128)(2,1)}, bf16[256,256]{1,0:T(8,128)(2,1)S(1)}, u32[]{:S(2)}, u32[]{:S(2)}) collective-permute-start(bf16[256,256]{1,0:T(8,128)(2,1)} %get-tuple-element.28), channel_id=1, source_target_pairs={{0,16},{16,32},{32,48},{48,64},{64,80},{80,96},{96,112},{112,0},{1... | collective-permute-start | bytes 393224 | tf_op jit(solution)/shard_map/ppermute | solution.py:358
  124.3 27.3 %collective-permute-start.33 = (bf16[256,256]{1,0:T(8,128)(2,1)}, bf16[256,256]{1,0:T(8,128)(2,1)S(1)}, u32[]{:S(2)}, u32[]{:S(2)}) collective-permute-start(bf16[256,256]{1,0:T(8,128)(2,1)} %get-tuple-element.29), channel_id=1, source_target_pairs={{0,112},{16,0},{32,16},{48,32},{64,48},{80,64},{96,80},{112,96},{1... | collective-permute-start | bytes 393224 | tf_op jit(solution)/shard_map/ppermute | solution.py:358
  138.1 5.9 %collective-permute-start.36 = (bf16[256,256]{1,0:T(8,128)(2,1)S(1)}, bf16[256,256]{1,0:T(8,128)(2,1)S(1)}, u32[]{:S(2)}, u32[]{:S(2)}) collective-permute-start(bf16[256,256]{1,0:T(8,128)(2,1)S(1)} %get-tuple-element.33), channel_id=1, source_target_pairs={{0,112},{16,0},{32,16},{48,32},{64,48},{80,64},{96,80},{112,96},{1... | collective-permute-start | bytes 393224 | tf_op jit(solution)/shard_map/ppermute | solution.py:358
  140.1 15.4 %collective-permute-start.38 = (bf16[256,256]{1,0:T(8,128)(2,1)}, bf16[256,256]{1,0:T(8,128)(2,1)S(1)}, u32[]{:S(2)}, u32[]{:S(2)}) collective-permute-start(bf16[256,256]{1,0:T(8,128)(2,1)} %get-tuple-element.34), channel_id=1, source_target_pairs={{0,64},{16,80},{32,96},{48,112},{64,0},{80,16},{96,32},{112,48},{1... | collective-permute-start | bytes 393224 | tf_op jit(solution)/shard_map/ppermute | solution.py:358
  141.0 18.3 %collective-permute-start.35 = (bf16[256,256]{1,0:T(8,128)(2,1)S(1)}, bf16[256,256]{1,0:T(8,128)(2,1)S(1)}, u32[]{:S(2)}, u32[]{:S(2)}) collective-permute-start(bf16[256,256]{1,0:T(8,128)(2,1)S(1)} %add_convert_fusion.3), channel_id=1, source_target_pairs={{0,32},{16,48},{32,64},{48,80},{64,96},{80,112},{96,0},{112,16},{1... | collective-permute-start | bytes 393224 | tf_op jit(solution)/shard_map/ppermute | solution.py:358
  144.0 15.2 %collective-permute-start.37 = (bf16[256,256]{1,0:T(8,128)(2,1)S(1)}, bf16[256,256]{1,0:T(8,128)(2,1)S(1)}, u32[]{:S(2)}, u32[]{:S(2)}) collective-permute-start(bf16[256,256]{1,0:T(8,128)(2,1)S(1)} %add_convert_fusion.2), channel_id=1, source_target_pairs={{0,96},{16,112},{32,0},{48,16},{64,32},{80,48},{96,64},{112,80},{1... | collective-permute-start | bytes 393224 | tf_op jit(solution)/shard_map/ppermute | solution.py:358
  146.6 13.5 %collective-permute-start.28 = (bf16[256,512]{1,0:T(8,128)(2,1)S(1)}, bf16[256,512]{1,0:T(8,128)(2,1)S(1)}, u32[]{:S(2)}, u32[]{:S(2)}) collective-permute-start(bf16[256,512]{1,0:T(8,128)(2,1)S(1)} %get-tuple-element.24), channel_id=1, source_target_pairs={{0,4},{4,8},{8,12},{12,0},{1,5},{5,9},{9,13},{13,1},{2,6},{6,10},{... | collective-permute-start | bytes 786440 | tf_op jit(solution)/shard_map/ppermute | solution.py:358
  151.6 11.0 %collective-permute-start.29 = (bf16[256,512]{1,0:T(8,128)(2,1)S(1)}, bf16[256,512]{1,0:T(8,128)(2,1)S(1)}, u32[]{:S(2)}, u32[]{:S(2)}) collective-permute-start(bf16[256,512]{1,0:T(8,128)(2,1)S(1)} %get-tuple-element.25), channel_id=1, source_target_pairs={{0,8},{4,12},{8,0},{12,4},{1,9},{5,13},{9,1},{13,5},{2,10},{6,14},... | collective-permute-start | bytes 786440 | tf_op jit(solution)/shard_map/ppermute | solution.py:358
  155.5 7.7 %collective-permute-start.30 = (bf16[256,512]{1,0:T(8,128)(2,1)S(1)}, bf16[256,512]{1,0:T(8,128)(2,1)S(1)}, u32[]{:S(2)}, u32[]{:S(2)}) collective-permute-start(bf16[256,512]{1,0:T(8,128)(2,1)S(1)} %get-tuple-element.26), channel_id=1, source_target_pairs={{0,12},{4,0},{8,4},{12,8},{1,13},{5,1},{9,5},{13,9},{2,14},{6,2},{... | collective-permute-start | bytes 786440 | tf_op jit(solution)/shard_map/ppermute | solution.py:358
  159.4 4.6 %collective-permute-start.39 = (bf16[128,256]{1,0:T(8,128)(2,1)S(1)}, bf16[128,256]{1,0:T(8,128)(2,1)S(1)}, u32[]{:S(2)}, u32[]{:S(2)}) collective-permute-start(bf16[128,256]{1,0:T(8,128)(2,1)S(1)} %slice.38), channel_id=1, source_target_pairs={{0,128},{128,0},{1,129},{129,1},{2,130},{130,2},{3,131},{131,3},{4... | collective-permute-start | bytes 196616 | tf_op jit(solution)/shard_map/ppermute | solution.py:358
  163.3 5.1 %collective-permute-start.31 = (bf16[128,512]{1,0:T(8,128)(2,1)S(1)}, bf16[128,512]{1,0:T(8,128)(2,1)S(1)}, u32[]{:S(2)}, u32[]{:S(2)}) collective-permute-start(bf16[128,512]{1,0:T(8,128)(2,1)S(1)} %get-tuple-element.36), channel_id=1, source_target_pairs={{0,128},{128,0},{1,129},{129,1},{2,130},{130,2},{3,131},{131,3},{4... | collective-permute-start | bytes 393224 | tf_op jit(solution)/shard_map/ppermute | solution.py:358
  (2 other events, 1.8 us)

commit v2 on v1

v2 whole, which is shorter than its diff:
```python
import functools
import math

import jax
import jax.numpy as jnp
from jax import lax
from jax.experimental import pallas as pl
from jax.experimental.pallas import tpu as pltpu
from jax.sharding import Mesh, PartitionSpec as P

HEAD = 128
RATIO = 4
CHUNK = 128
XL, NZ, NY = 2, 8, 4
HALF = NZ * NY * CHUNK
PLANE = NY * CHUNK
PIECE = CHUNK + 16
KEYS = NZ * CHUNK
KT = 256
ROWS = 1024
PAIRS = 4
GROUP = RATIO * HEAD
SCALE = HEAD**-0.5
C2 = SCALE * math.log2(math.e)
NEG = -1e30
WIDE = jnp.float32
LOW = jnp.bfloat16
NT = (((1,), (1,)), ((), ()))
NN = (((1,), (0,)), ((), ()))
VMEM_LIMIT = 48 * 1024 * 1024


def dot(a, b, dims=NN):
    return lax.dot_general(a, b, dims, preferred_element_type=WIDE)


def vspec():
    return pl.BlockSpec(memory_space=pltpu.VMEM)


def sspec():
    return pl.BlockSpec(memory_space=pltpu.SMEM)


def params():
    return pltpu.CompilerParams(vmem_limit_bytes=VMEM_LIMIT)


def up_first(pos, own, mate, weight):
    def kernel(pos_ref, g0, g1, w_ref, out_ref):
        @pl.when(pl.program_id(0) == 0)
        def _():
            out_ref[...] = dot(g0[...], w_ref[...])

        @pl.when(pl.program_id(0) == 1)
        def _():
            out_ref[...] += dot(g1[...], w_ref[...])

    full = pl.BlockSpec((CHUNK, 1024), lambda r, pos: (0, 0))
    return pl.pallas_call(
        kernel,
        grid_spec=pltpu.PrefetchScalarGridSpec(
            num_scalar_prefetch=1,
            grid=(2,),
            in_specs=[
                full,
                full,
                pl.BlockSpec((1024, 1024), lambda r, pos: (jnp.bitwise_xor(pos[0], r), 0)),
            ],
            out_specs=pl.BlockSpec((CHUNK, 1024), lambda r, pos: (0, 0)),
        ),
        out_shape=jax.ShapeDtypeStruct((CHUNK, 1024), WIDE),
        compiler_params=params(),
        name="upstream_first",
    )(pos, own, mate, weight)


def up_second(pos, part, far, far_mate, weight):
    def kernel(pos_ref, part_ref, g0, g1, w_ref, own_ref, oth_ref, acc):
        @pl.when(pl.program_id(0) == 0)
        def _():
            acc[...] = part_ref[...] + dot(g0[...], w_ref[...])

        @pl.when(pl.program_id(0) == 1)
        def _():
            acc[...] += dot(g1[...], w_ref[...])
            xl = pos_ref[1]
            own_ref[...] = acc[:, pl.ds(pl.multiple_of(xl * GROUP, GROUP), GROUP)].astype(LOW)
            oth_ref[...] = acc[:, pl.ds(pl.multiple_of((1 - xl) * GROUP, GROUP), GROUP)].astype(LOW)

    full = pl.BlockSpec((CHUNK, 1024), lambda r, pos: (0, 0))
    half = pl.BlockSpec((CHUNK, GROUP), lambda r, pos: (0, 0))
    return pl.pallas_call(
        kernel,
        grid_spec=pltpu.PrefetchScalarGridSpec(
            num_scalar_prefetch=1,
            grid=(2,),
            in_specs=[
                full,
                full,
                full,
                pl.BlockSpec((1024, 1024), lambda r, pos: (jnp.bitwise_xor(pos[0], 2 + r), 0)),
            ],
            out_specs=[half, half],
            scratch_shapes=[pltpu.VMEM((CHUNK, 1024), WIDE)],
        ),
        out_shape=[jax.ShapeDtypeStruct((CHUNK, GROUP), LOW)] * 2,
        compiler_params=params(),
        name="upstream_second",
    )(pos, part, far, far_mate, weight)


def stack_rows(dst, blocks, step):
    for o in range(2):
        for dy in range(NY):
            for h in range(RATIO):
                start = (dy % 2) * GROUP + h * CHUNK
                dst[o * 2 + dy // 2, start : start + CHUNK, :] = blocks[dy][
                    o * step : o * step + CHUNK, h * HEAD : (h + 1) * HEAD
                ]


def key_chunk(xl, z, o, d):
    plane = lax.rem(z + d, NZ)
    if o == 0:
        return xl * 4 + plane // 2
    return (1 - xl) * 4 + (NZ - 1 - plane) // 2


def count_row(ref, o):
    at = o * PIECE + CHUNK
    return ref[at : at + 16, :HEAD].astype(WIDE)[:1]


def fill_low(low_s, q, kv):
    zeros = sum(count_row(ref, o) for ref in kv for o in range(2))
    tok = lax.broadcasted_iota(jnp.int32, (1, CHUNK), 1).astype(WIDE)
    for o in range(2):
        for dy in range(NY):
            low = jnp.where(tok >= count_row(q[dy], o), zeros, 0.0)
            for h in range(RATIO):
                start = (dy % 2) * GROUP + h * CHUNK
                pair = o * 2 + dy // 2
                low_s[pair : pair + 1, start : start + CHUNK] = low


def row_limits(cls, pair, xl, z, y, low_s):
    o = pair // 2
    h = jnp.where(o == 0, xl, 1 - xl)
    plane = jnp.where(o == 0, z, NZ - 1 - z)
    dy0 = (pair % 2) * 2
    y0 = lax.rem(y + dy0, NY)
    y1 = lax.rem(y + dy0 + 1, NY)
    parity = lax.rem(plane + cls, 2)
    full = h * (KEYS // 2) + ((plane + 1 - parity) // 2) * CHUNK
    if cls == 0:
        lane = lax.broadcasted_iota(jnp.int32, (1, ROWS), 1)
        off = jnp.where(lane < GROUP, y0, y1) * CHUNK + jnp.bitwise_and(lane, CHUNK - 1)
        high = full + jnp.clip(off - y * CHUNK + 1, 0, CHUNK)
        top = full + jnp.where(jnp.maximum(y0, y1) >= y, CHUNK, 0)
    else:
        high = jnp.full((1, ROWS), full, jnp.int32)
        top = full
    low_f = low_s[pl.ds(pair, 1), :]
    low = low_f.astype(jnp.int32)
    t_low = jnp.min(low_f).astype(jnp.int32) // KT
    t_high = (top + KT - 1) // KT
    return low, high, t_low, t_high


def masked_scores(k, q, t, low, high):
    s = dot(k, q, NT) * C2
    kk = t * KT + lax.broadcasted_iota(jnp.int32, (KT, ROWS), 0)
    return jnp.where((kk >= low) & (kk < high), s, NEG)


def forward(cls, scalars, q_blocks, kv_views):
    def kernel(sc, *refs):
        q = refs[0:4]
        kv = refs[4:8]
        o_ref, ml_ref, qs, kc, vt, low_s = refs[8:]
        xl, z, y = sc[0], sc[1], sc[2]
        stack_rows(qs, q, PIECE)
        fill_low(low_s, q, kv)
        for i in range(4):
            for o in range(2):
                at = key_chunk(xl, z, o, 2 * i + cls)
                rows = slice(o * PIECE, o * PIECE + CHUNK)
                kc[at] = kv[i][rows, :HEAD]
                vt[at, :HEAD, :] = kv[i][rows, HEAD:].T
                vt[at, HEAD:, :] = jnp.ones((16, CHUNK), LOW)

        def one_pair(pair, _):
            low, high, t_low, t_high = row_limits(cls, pair, xl, z, y, low_s)
            o_ref[pair] = jnp.zeros((HEAD + 16, ROWS), WIDE)
            qp = qs[pair]

            def tile(t, top):
                k = kc[pl.ds(2 * t, 2)].reshape(KT, HEAD)
                s = masked_scores(k, qp, t, low, high)
                new = jnp.maximum(top, jnp.max(s, axis=0, keepdims=True))
                p = jnp.exp2(s - new).astype(LOW)
                v = jnp.concatenate([vt[2 * t], vt[2 * t + 1]], axis=1)
                o_ref[pair] = o_ref[pair] * jnp.exp2(top - new) + dot(v, p)
                return new

            top = lax.fori_loop(t_low, t_high, tile, jnp.full((1, ROWS), NEG, WIDE))
            ml_ref[pl.ds(pair, 1), :] = top
            return 0

        lax.fori_loop(0, PAIRS, one_pair, 0)
        for pair in range(PAIRS):
            ml_ref[PAIRS + pair : PAIRS + pair + 1, :] = o_ref[pair, HEAD : HEAD + 1, :]

    return pl.pallas_call(
        kernel,
        grid=(1,),
        in_specs=[sspec()] + [vspec()] * 4 + [view_spec(i) for _, i in kv_views],
        out_specs=[vspec()] * 2,
        out_shape=[
            jax.ShapeDtypeStruct((PAIRS, HEAD + 16, ROWS), WIDE),
            jax.ShapeDtypeStruct((2 * PAIRS, ROWS), WIDE),
        ],
        scratch_shapes=[
            pltpu.VMEM((PAIRS, ROWS, HEAD), LOW),
            pltpu.VMEM((NZ, CHUNK, HEAD), LOW),
            pltpu.VMEM((NZ, HEAD + 16, CHUNK), LOW),
            pltpu.VMEM((PAIRS, ROWS), WIDE),
        ],
        compiler_params=params(),
        cost_estimate=pl.CostEstimate(
            flops=4 * 10**9, bytes_accessed=4 * 2**20, transcendentals=2 * 2**20
        ),
        name="forward%d" % cls,
    )(scalars, *q_blocks, *[a for a, _ in kv_views])


def view_spec(i):
    return pl.BlockSpec((2 * PIECE, 2 * HEAD), lambda s: (i, 0))


def weighted(parts, u_blocks):
    def kernel(o0, ml0, o1, ml1, *refs):
        u = refs[0:4]
        out_ref = refs[4]
        top = jnp.maximum(ml0[:PAIRS], ml1[:PAIRS])
        f0 = jnp.exp2(ml0[:PAIRS] - top)
        f1 = jnp.exp2(ml1[:PAIRS] - top)
        out_ref[:PAIRS, :] = top
        out_ref[PAIRS : 2 * PAIRS, :] = f0 * ml0[PAIRS:] + f1 * ml1[PAIRS:]
        for o in range(2):
            for dy in range(NY):
                pair = o * 2 + dy // 2
                for h in range(RATIO):
                    start = (dy % 2) * GROUP + h * CHUNK
                    at = slice(start, start + CHUNK)
                    ut = u[dy][o * CHUNK : (o + 1) * CHUNK, h * HEAD : (h + 1) * HEAD]
                    ut = ut.astype(WIDE).T
                    one = jnp.sum(ut * o0[pair, :HEAD, at], axis=0, keepdims=True)
                    two = jnp.sum(ut * o1[pair, :HEAD, at], axis=0, keepdims=True)
                    out_ref[2 * PAIRS + pair : 2 * PAIRS + pair + 1, at] = (
                        f0[pair : pair + 1, at] * one + f1[pair : pair + 1, at] * two
                    )

    return pl.pallas_call(
        kernel,
        in_specs=[vspec()] * 8,
        out_specs=vspec(),
        out_shape=jax.ShapeDtypeStruct((3 * PAIRS, ROWS), WIDE),
        compiler_params=params(),
        name="weighted",
    )(*parts[0], *parts[1], *u_blocks)


def backward(cls, scalars, stats, q_blocks, u_blocks, kv_views, dq_before):
    last = dq_before is not None

    def kernel(sc, *refs):
        st = refs[0:4]
        q = refs[4:8]
        u = refs[8:12]
        kv = refs[12:16]
        refs = refs[16:]
        if last:
            before, refs = refs[0], refs[1:]
            dq_out, dkv_out, refs = refs[0:4], refs[4:8], refs[8:]
        else:
            dq_out, dkv_out, refs = refs[0:1], refs[1:3], refs[3:]
        qs, us, kc, vc, kt, dk, dv, al, lse_s, delta_s, low_s = refs[:11]
        dqt = refs[11] if last else dq_out[0]
        xl, z, y = sc[0], sc[1], sc[2]
        stack_rows(qs, q, PIECE)
        stack_rows(us, u, CHUNK)
        fill_low(low_s, q, kv)
        for i in range(4):
            for o in range(2):
                at = key_chunk(xl, z, o, 2 * i + cls)
                rows = slice(o * PIECE, o * PIECE + CHUNK)
                key = kv[i][rows, :HEAD]
                kc[at] = key
                vc[at] = kv[i][rows, HEAD:]
                kt[at] = key.T
        dk[...] = jnp.zeros(dk.shape, WIDE)
        dv[...] = jnp.zeros(dv.shape, WIDE)
        dqt[...] = before[...] if last else jnp.zeros(dqt.shape, WIDE)

        for i in range(NY):
            for row in range(0, 3 * PAIRS, 2):
                for dy in range(NY):
                    e = (dy - i) % NY
                    to, frm = (dy % 2) * GROUP, (e % 2) * GROUP
                    al[i, row + dy // 2 : row + dy // 2 + 1, to : to + GROUP] = st[i][
                        row + e // 2 : row + e // 2 + 1, frm : frm + GROUP
                    ]
        tops = [al[i, :PAIRS] for i in range(NY)]
        top = functools.reduce(jnp.maximum, tops)
        factors = [jnp.exp2(t - top) for t in tops]
        mass = sum(f * al[i, PAIRS : 2 * PAIRS] for i, f in enumerate(factors))
        share = sum(f * al[i, 2 * PAIRS :] for i, f in enumerate(factors))
        lse_s[...] = top + jnp.log2(mass)
        delta_s[...] = share / mass

        def one_pair(pair, _):
            low, high, t_low, t_high = row_limits(cls, pair, xl, z, y, low_s)
            lse = lse_s[pl.ds(pair, 1), :]
            delta = delta_s[pl.ds(pair, 1), :]
            qp = qs[pair]
            up = us[pair]

            def tile(t, _):
                k = kc[pl.ds(2 * t, 2)].reshape(KT, HEAD)
                v = vc[pl.ds(2 * t, 2)].reshape(KT, HEAD)
                p = jnp.exp2(masked_scores(k, qp, t, low, high) - lse)
                ds = (p * (dot(v, up, NT) - delta)).astype(LOW)
                p = p.astype(LOW)
                dv[pl.ds(2 * t, 2)] += dot(p, up).reshape(2, CHUNK, HEAD)
                dk[pl.ds(2 * t, 2)] += dot(ds, qp).reshape(2, CHUNK, HEAD)
                kt_tile = jnp.concatenate([kt[2 * t], kt[2 * t + 1]], axis=1)
                dqt[pair] += dot(kt_tile, ds)
                return 0

            lax.fori_loop(t_low, t_high, tile, 0)
            return 0

        lax.fori_loop(0, PAIRS, one_pair, 0)

        def write(out, first, d):
            for o in range(2):
                at = key_chunk(xl, z, o, d)
                rows = slice(first + o * CHUNK, first + (o + 1) * CHUNK)
                out[rows, :HEAD] = (dk[at] * SCALE).astype(out.dtype)
                out[rows, HEAD:] = dv[at].astype(out.dtype)

        if last:
            for i in range(4):
                write(dkv_out[i], 0, 2 * i)
            for dy in range(NY):
                for o in range(2):
                    for h in range(RATIO):
                        start = (dy % 2) * GROUP + h * CHUNK
                        part = dqt[o * 2 + dy // 2, :, start : start + CHUNK].T * SCALE
                        dq_out[dy][
                            o * CHUNK : (o + 1) * CHUNK, h * HEAD : (h + 1) * HEAD
                        ] = part.astype(dq_out[dy].dtype)
        else:
            write(dkv_out[0], 0, 1)
            write(dkv_out[0], 2 * CHUNK, 3)
            write(dkv_out[1], 0, 7)
            write(dkv_out[1], 2 * CHUNK, 5)

    dq_state = jax.ShapeDtypeStruct((PAIRS, HEAD, ROWS), WIDE)
    if last:
        out_shape = [
            jax.ShapeDtypeStruct((2 * CHUNK, GROUP), WIDE if dy == 0 else LOW)
            for dy in range(NY)
        ] + [
            jax.ShapeDtypeStruct((2 * CHUNK, 2 * HEAD), LOW if i == 2 else WIDE)
            for i in range(4)
        ]
    else:
        out_shape = [dq_state] + [jax.ShapeDtypeStruct((4 * CHUNK, 2 * HEAD), LOW)] * 2
    state = [dq_before] if last else []
    return pl.pallas_call(
        kernel,
        grid=(1,),
        in_specs=[sspec()]
        + [vspec()] * 12
        + [view_spec(i) for _, i in kv_views]
        + [vspec()] * len(state),
        out_specs=[vspec()] * len(out_shape),
        out_shape=out_shape,
        scratch_shapes=[
            pltpu.VMEM((PAIRS, ROWS, HEAD), LOW),
            pltpu.VMEM((PAIRS, ROWS, HEAD), LOW),
            pltpu.VMEM((NZ, CHUNK, HEAD), LOW),
            pltpu.VMEM((NZ, CHUNK, HEAD), LOW),
            pltpu.VMEM((NZ, HEAD, CHUNK), LOW),
            pltpu.VMEM((NZ, CHUNK, HEAD), WIDE),
            pltpu.VMEM((NZ, CHUNK, HEAD), WIDE),
            pltpu.VMEM((NY, 3 * PAIRS, ROWS), WIDE),
            pltpu.VMEM((PAIRS, ROWS), WIDE),
            pltpu.VMEM((PAIRS, ROWS), WIDE),
            pltpu.VMEM((PAIRS, ROWS), WIDE),
        ]
        + ([pltpu.VMEM((PAIRS, HEAD, ROWS), WIDE)] if last else []),
        compiler_params=params(),
        cost_estimate=pl.CostEstimate(
            flops=8 * 10**9, bytes_accessed=6 * 2**20, transcendentals=2 * 2**20
        ),
        name="backward%d" % cls,
    )(scalars, *stats, *q_blocks, *u_blocks, *[a for a, _ in kv_views], *state)


def shift(x, axis, size, d):
    return lax.ppermute(x, axis, [(i, (i - d) % size) for i in range(size)])


def swap(x):
    last = XL * NZ - 1
    return lax.ppermute(x, ("xl", "z"), [(i, last - i) for i in range(last + 1)])


def per_device(queries, keys, values, grad_out, out_weight, segments):
    xl, z, y = lax.axis_index("xl"), lax.axis_index("z"), lax.axis_index("y")
    tp = lax.axis_index("xh") * 2 + lax.axis_index("core")

    def part(x, group, width):
        return lax.dynamic_slice_in_dim(x, group * width, width, 1)

    count = jnp.sum((segments == 0).astype(WIDE)).astype(LOW)

    def key_value(group):
        both = jnp.concatenate([part(keys, group, HEAD), part(values, group, HEAD)], axis=1)
        return jnp.concatenate([both, jnp.full((16, 2 * HEAD), count, LOW)], axis=0)

    def query(group):
        return jnp.concatenate([part(queries, group, GROUP), jnp.full((16, GROUP), count, LOW)], axis=0)

    pos = jnp.stack([tp, xl]).astype(jnp.int32)
    scalars = jnp.stack([xl, z, y]).astype(jnp.int32)
    kv_in = swap(key_value(1 - xl))
    q_in = swap(query(1 - xl))
    far = shift(grad_out, "xh", 2, 1)
    mate = shift(grad_out, "core", 2, 1)

    def along_y(x):
        return [x] + [shift(x, "y", NY, d) for d in (1, 2, 3)]

    kv = jnp.concatenate([key_value(xl), kv_in], axis=0)
    kv_up2 = shift(kv, "z", NZ, 2)
    kv_down2 = shift(kv, "z", NZ, -2)
    kv_4 = shift(kv, "z", NZ, 4)
    q_blocks = along_y(jnp.concatenate([query(xl), q_in], axis=0))
    kv_up = shift(jnp.concatenate([kv, kv_up2], axis=0), "z", NZ, 1)
    kv_down = shift(jnp.concatenate([kv, kv_down2], axis=0), "z", NZ, -1)
    even = [(kv, 0), (kv_up2, 0), (kv_4, 0), (kv_down2, 0)]
    odd = [(kv_up, 0), (kv_up, 1), (kv_down, 1), (kv_down, 0)]

    u_part = up_first(pos, grad_out, mate, out_weight)
    far_mate = shift(far, "core", 2, 1)
    u_own, u_oth = up_second(pos, u_part, far, far_mate, out_weight)
    u_blocks = along_y(jnp.concatenate([u_own, swap(u_oth)], axis=0))

    parts = [forward(0, scalars, q_blocks, even), forward(1, scalars, q_blocks, odd)]
    stats = along_y(weighted(parts, u_blocks))
    dq_state, bundle_up, bundle_down = backward(
        1, scalars, stats, q_blocks, u_blocks, odd, None
    )
    got_up = shift(bundle_up, "z", NZ, -1)
    got_down = shift(bundle_down, "z", NZ, 1)
    *dq, dkv, dkv_up2, dkv_4, dkv_down2 = backward(
        0, scalars, stats, q_blocks, u_blocks, even, dq_state
    )

    near, further = slice(0, 2 * CHUNK), slice(2 * CHUNK, None)
    dkv = dkv + got_up[near].astype(WIDE) + got_down[near].astype(WIDE)
    up2 = (dkv_up2 + got_up[further].astype(WIDE)).astype(LOW)
    down2 = (dkv_down2 + got_down[further].astype(WIDE)).astype(LOW)
    for g in (
        shift(dkv_4, "z", NZ, 4),
        shift(up2, "z", NZ, -2),
        shift(down2, "z", NZ, 2),
    ):
        dkv = dkv + g.astype(WIDE)

    dq_sum = dq[0]
    for d in (1, 2, 3):
        dq_sum = dq_sum + shift(dq[d], "y", NY, -d).astype(WIDE)

    dq_back = swap(dq_sum[CHUNK:].astype(LOW))
    dkv_back = swap(dkv[CHUNK:].astype(LOW))
    dq_own = dq_sum[:CHUNK].astype(LOW)
    dkv_own = dkv[:CHUNK].astype(LOW)

    def join(a, c):
        return jnp.where(
            xl == 0, jnp.concatenate([a, c], axis=1), jnp.concatenate([c, a], axis=1)
        )

    return (
        join(dq_own, dq_back),
        join(dkv_own[:, :HEAD], dkv_back[:, :HEAD]),
        join(dkv_own[:, HEAD:], dkv_back[:, HEAD:]),
    )


def solution(mesh):
    fine = Mesh(mesh.devices.reshape(XL, NZ, NY, 2, 2), ("xl", "z", "y", "xh", "core"))
    ctx, tp = ("xl", "z", "y"), ("xh", "core")
    in_specs = (P(ctx, tp), P(ctx, tp), P(ctx, tp), P(ctx, tp), P(None, tp), P(ctx))
    out_specs = (P(ctx, tp), P(ctx, tp), P(ctx, tp))
    return jax.shard_map(
        per_device, mesh=fine, in_specs=in_specs, out_specs=out_specs, check_vma=False
    )
```

time: 167 us -> 150 us (0.90)
  starting transfers between devices: 90.3 us -> 55.3 us
  blocking collectives: 21.8 us -> 0 us
  waiting for transfers between devices: 17.8 us -> 38.6 us
  Pallas kernels: 28.2 us -> 46.1 us
    ppermute x40 -> x25, starting transfers between devices: 90.3 us -> 44.2 us  [shift(): return lax.ppermute(x, axis, [(i, (i - d) % size) for i in range(size)])]
    psum x1 -> x0, blocking collectives: 21.8 us -> none  [per_device(): lax.psum(jnp.sum((segments == 0).astype(jnp.int32)), ('xl', 'z', 'y'))]
    pallas_call x3 -> x5, Pallas kernels: 21.7 us -> 39.5 us  [the longest x2 23.3 us: backward(): pl.pallas_call(kernel, grid=(1,), in_specs=[sspec()] + [vspec()] * 12 + [...]
    ppermute x40 -> x25, waiting for transfers between devices: 17.8 us -> 30.7 us  [shift(): return lax.ppermute(x, axis, [(i, (i - d) % size) for i in range(size)])]
    ppermute x0 -> x5, starting transfers between devices: none -> 11.1 us  [swap(): lax.ppermute(x, ('xl', 'z'), [(i, last - i) for i in range(last + 1)])]
    ppermute x0 -> x5, waiting for transfers between devices: none -> 7.87 us  [swap(): lax.ppermute(x, ('xl', 'z'), [(i, last - i) for i in range(last + 1)])]
    unnamed x20 -> x5, local copies, waits for them, and re-layouts: 4.58 us -> 1.37 us
  transfers between devices with their start and end apart: 40 -> 30, of which waited for: 10 -> 13; matrix products, arithmetic and copies ran while one was open for 3% -> 3% of each run, Pallas kernels for 9% -> 24%
where the time goes in v2:
time: 150 us; the launch traced here: 151 us
  starting transfers between devices  55.3 us (37%)
  Pallas kernels  46.1 us (31%)
  waiting for transfers between devices  38.6 us (26%)
  local copies, waits for them, and re-layouts  5.18 us (3%)
  other arithmetic  4.64 us (3%)
    ppermute x25, starting transfers between devices, shift(): return lax.ppermute(x, axis, [(i, (i - d) % size) for i in range(size)])  44.2 us
    ppermute x25, waiting for transfers between devices, shift(): return lax.ppermute(x, axis, [(i, (i - d) % size) for i in range(size)])  30.7 us
    pallas_call x2, Pallas kernels, backward(): pl.pallas_call(kernel, grid=(1,), in_specs=[sspec()] + [vspec()] * 12 + [...  23.3 us
    pallas_call x2, Pallas kernels, forward(): pl.pallas_call(kernel, grid=(1,), in_specs=[sspec()] + [vspec()] * 4 + [v...  15.7 us
    ppermute x5, starting transfers between devices, swap(): lax.ppermute(x, ('xl', 'z'), [(i, last - i) for i in range(last + 1)])  11.1 us
    ppermute x5, waiting for transfers between devices, swap(): lax.ppermute(x, ('xl', 'z'), [(i, last - i) for i in range(last + 1)])  7.87 us
    pallas_call x1, Pallas kernels, up_second(): pl.pallas_call(kernel, grid_spec=pltpu.PrefetchScalarGridSpec(num_scalar_...  3.28 us
    pallas_call x1, Pallas kernels, up_first(): pl.pallas_call(kernel, grid_spec=pltpu.PrefetchScalarGridSpec(num_scalar_...  3.25 us
  transfers between devices with their start and end apart: 30, of which 13 were waited for; matrix products, arithmetic and copies ran while one was open for 3% of the time, Pallas kernels for 24%

profile of v2, /device:TPU:2, one launch (start us, length us, event | category | flops | bytes accessed | tf_op | source)
XLA Modules:
  0.0 150.6 jit_solution(14156365970959146466)
XLA Ops:
  0.6 1.3 fusion.3
  2.0 0.8 constant_dynamic-slice_fusion.2
  2.8 0.7 fusion.2
  3.4 5.9 %collective-permute-start.4 = (bf16[144,256]{1,0:T(8,128)(2,1)S(1)}, bf16[144,256]{1,0:T(8,128)(2,1)S(1)}, u32[]{:S(2)}, u32[]{:S(2)}) collective-permute-start(bf16[144,256]{1,0:T(8,128)(2,1)S(1)} %fusion.2), channel_id=1, source_target_pairs={{0,240},{16,224},{32,208},{48,192},{64,176},{80,160},{96,144},{112... | collective-permute-start | bytes 221192 | tf_op jit(solution)/shard_map/ppermute | solution.py:420
  9.4 1.0 constant_dynamic-slice_fusion.5
  10.3 0.7 concatenate.47
  11.2 2.5 %collective-permute-start.11 = (bf16[128,1024]{1,0:T(8,128)(2,1)}, bf16[128,1024]{1,0:T(8,128)(2,1)S(1)}, u32[]{:S(2)}, u32[]{:S(2)}) collective-permute-start(bf16[128,1024]{1,0:T(8,128)(2,1)} %g0.1), channel_id=1, source_target_pairs={{0,2},{2,0},{1,3},{3,1},{4,6},{6,4},{5,7},{7,5},{8,10},{10,8},{9,1... | collective-permute-start | bytes 786440 | tf_op jit(solution)/shard_map/ppermute | solution.py:415
  13.7 0.6 broadcast_in_dim.8
  14.4 1.9 %collective-permute-done.4 = bf16[144,256]{1,0:T(8,128)(2,1)S(1)} collective-permute-done((bf16[144,256]{1,0:T(8,128)(2,1)S(1)}, bf16[144,256]{1,0:T(8,128)(2,1)S(1)}, u32[]{:S(2)}, u32[]{:S(2)}) %collective-permute-start.4) | collective-permute-done | bytes 73760 | tf_op jit(solution)/shard_map/ppermute | solution.py:420
  16.3 0.6 broadcast_in_dim.9
  17.0 1.1 collective-permute-start.7
  18.0 3.2 %collective-permute-start.5 = (bf16[288,256]{1,0:T(8,128)(2,1)S(1)}, bf16[288,256]{1,0:T(8,128)(2,1)S(1)}, u32[]{:S(2)}, u32[]{:S(2)}) collective-permute-start(bf16[288,256]{1,0:T(8,128)(2,1)S(1)} %pad_maximum_fusion.4.refs_4_.refs_12_), channel_id=1, source_target_pairs={{0,96},{16,112},{32,0},{48,16},{64,32},{80,48},{96,64},{112,80},{1... | collective-permute-start | bytes 442376 | tf_op jit(solution)/shard_map/ppermute | solution.py:415
  21.9 1.7 %collective-permute-start.3 = (bf16[288,512]{1,0:T(8,128)(2,1)S(1)}, bf16[288,512]{1,0:T(8,128)(2,1)S(1)}, u32[]{:S(2)}, u32[]{:S(2)}) collective-permute-start(bf16[288,512]{1,0:T(8,128)(2,1)S(1)} %pad_maximum_fusion.refs_0_.refs_4_), channel_id=1, source_target_pairs={{0,4},{4,8},{8,12},{12,0},{1,5},{5,9},{9,13},{13,1},{2,6},{6,10},{... | collective-permute-start | bytes 884744 | tf_op jit(solution)/shard_map/ppermute | solution.py:415
  23.5 3.8 %collective-permute-done.7.refs_7_.refs_15_ = bf16[288,256]{1,0:T(8,128)(2,1)S(1)} collective-permute-done((bf16[288,256]{1,0:T(8,128)(2,1)S(1)}, bf16[288,256]{1,0:T(8,128)(2,1)S(1)}, u32[]{:S(2)}, u32[]{:S(2)}) %collective-permute-start.7) | collective-permute-done | bytes 147488 | tf_op jit(solution)/shard_map/ppermute | solution.py:415
  27.3 3.2 %collective-permute-start.2 = (bf16[288,512]{1,0:T(8,128)(2,1)S(1)}, bf16[288,512]{1,0:T(8,128)(2,1)S(1)}, u32[]{:S(2)}, u32[]{:S(2)}) collective-permute-start(bf16[288,512]{1,0:T(8,128)(2,1)S(1)} %pad_maximum_fusion.refs_0_.refs_4_), channel_id=1, source_target_pairs={{0,8},{4,12},{8,0},{12,4},{1,9},{5,13},{9,1},{13,5},{2,10},{6,14},... | collective-permute-start | bytes 884744 | tf_op jit(solution)/shard_map/ppermute | solution.py:415
  30.5 1.5 %collective-permute-start.1 = (bf16[288,512]{1,0:T(8,128)(2,1)S(1)}, bf16[288,512]{1,0:T(8,128)(2,1)S(1)}, u32[]{:S(2)}, u32[]{:S(2)}) collective-permute-start(bf16[288,512]{1,0:T(8,128)(2,1)S(1)} %pad_maximum_fusion.refs_0_.refs_4_), channel_id=1, source_target_pairs={{0,12},{4,0},{8,4},{12,8},{1,13},{5,1},{9,5},{13,9},{2,14},{6,2},{... | collective-permute-start | bytes 884744 | tf_op jit(solution)/shard_map/ppermute | solution.py:415
  32.1 3.0 %collective-permute-start.6 = (bf16[288,256]{1,0:T(8,128)(2,1)S(1)}, bf16[288,256]{1,0:T(8,128)(2,1)S(1)}, u32[]{:S(2)}, u32[]{:S(2)}) collective-permute-start(bf16[288,256]{1,0:T(8,128)(2,1)S(1)} %pad_maximum_fusion.4.refs_4_.refs_12_), channel_id=1, source_target_pairs={{0,64},{16,80},{32,96},{48,112},{64,0},{80,16},{96,32},{112,48},{1... | collective-permute-start | bytes 442376 | tf_op jit(solution)/shard_map/ppermute | solution.py:415
  35.2 3.3 %upstream_first.1.part_ref = f32[128,1024]{1,0:T(8,128)S(1)} custom-call(s32[2]{0:T(128)S(1)} %pad_add_fusion.1.pos_ref, bf16[128,1024]{1,0:T(8,128)(2,1)S(1)} %copy-done, bf16[128,1024]{1,0:T(8,128)(2,1)S(1)} %collective-permute-done.10.g1, bf16[4096,1024]{1,0:T(8,128)(2,1)} %w_ref.3), custom_call_target="tpu_custom_call" | custom-call | tf_op jit(solution)/shard_map/upstream_first/pallas_call | solution.py:60
  38.5 3.5 %collective-permute-start.9 = (bf16[576,256]{1,0:T(8,128)(2,1)S(1)}, bf16[576,256]{1,0:T(8,128)(2,1)S(1)}, u32[]{:S(2)}, u32[]{:S(2)}) collective-permute-start(bf16[576,256]{1,0:T(8,128)(2,1)S(1)} %get-tuple-element.41), channel_id=1, source_target_pairs={{0,16},{16,32},{32,48},{48,64},{64,80},{80,96},{96,112},{112,0},{1... | collective-permute-start | bytes 884744 | tf_op jit(solution)/shard_map/ppermute | solution.py:415
  42.0 3.3 %upstream_second.1 = (bf16[128,512]{1,0:T(8,128)(2,1)S(1)}, bf16[128,512]{1,0:T(8,128)(2,1)S(1)}) custom-call(s32[2]{0:T(128)S(1)} %pad_add_fusion.1.pos_ref, f32[128,1024]{1,0:T(8,128)S(1)} %upstream_first.1.part_ref, bf16[128,1024]{1,0:T(8,128)(2,1)S(1)} %collective-permute-done.11.g0, bf16[128,1024]{1,0:T(8,128)(2,1)S(1)} %collective-permute-done.12.g1, ...), custom_call_target="tpu_custom_call" | custom-call | tf_op jit(solution)/shard_map/upstream_second/pallas_call | solution.py:93
  45.3 2.1 %collective-permute-start.8 = (bf16[576,256]{1,0:T(8,128)(2,1)S(1)}, bf16[576,256]{1,0:T(8,128)(2,1)S(1)}, u32[]{:S(2)}, u32[]{:S(2)}) collective-permute-start(bf16[576,256]{1,0:T(8,128)(2,1)S(1)} %get-tuple-element.42), channel_id=1, source_target_pairs={{0,112},{16,0},{32,16},{48,32},{64,48},{80,64},{96,80},{112,96},{1... | collective-permute-start | bytes 884744 | tf_op jit(solution)/shard_map/ppermute | solution.py:415
  47.4 2.7 %collective-permute-start.13 = (bf16[128,512]{1,0:T(8,128)(2,1)S(1)}, bf16[128,512]{1,0:T(8,128)(2,1)S(1)}, u32[]{:S(2)}, u32[]{:S(2)}) collective-permute-start(bf16[128,512]{1,0:T(8,128)(2,1)S(1)} %get-tuple-element.25), channel_id=1, source_target_pairs={{0,240},{16,224},{32,208},{48,192},{64,176},{80,160},{96,144},{112... | collective-permute-start | bytes 393224 | tf_op jit(solution)/shard_map/ppermute | solution.py:420
  50.1 8.7 %forward0.1 = (f32[4,144,1024]{2,1,0:T(8,128)S(1)}, f32[8,1024]{1,0:T(8,128)S(1)}) custom-call(s32[3]{0:T(128)S(1)} %pad_add_fusion.sc, bf16[288,512]{1,0:T(8,128)(2,1)S(1)} %pad_maximum_fusion.refs_0_.refs_4_, bf16[288,512]{1,0:T(8,128)(2,1)S(1)} %collective-permute-done.1.refs_1_.refs_5_, bf16[288,512]{1,0:T(8,128)(2,1)S(1)} %collective-permute-done.2.refs_2_.refs_6_, ...), custom_call_target="tpu_custom_call" | custom-call | flops 4000000000 | bytes 4194304 | tf_op jit(solution)/shard_map/forward0/pallas_call | solution.py:215
  59.5 2.3 %collective-permute-start.15 = (bf16[256,512]{1,0:T(8,128)(2,1)S(1)}, bf16[256,512]{1,0:T(8,128)(2,1)S(1)}, u32[]{:S(2)}, u32[]{:S(2)}) collective-permute-start(bf16[256,512]{1,0:T(8,128)(2,1)S(1)} %constant_dynamic-update-slice_fusion.refs_0_.refs_8_), channel_id=1, source_target_pairs={{0,8},{4,12},{8,0},{12,4},{1,9},{5,13},{9,1},{13,5},{2,10},{6,14},... | collective-permute-start | bytes 786440 | tf_op jit(solution)/shard_map/ppermute | solution.py:415
  61.8 0.9 collective-permute-start.14
  62.7 7.1 %forward1.1 = (f32[4,144,1024]{2,1,0:T(8,128)S(1)}, f32[8,1024]{1,0:T(8,128)S(1)}) custom-call(s32[3]{0:T(128)S(1)} %pad_add_fusion.sc, bf16[288,512]{1,0:T(8,128)(2,1)S(1)} %pad_maximum_fusion.refs_0_.refs_4_, bf16[288,512]{1,0:T(8,128)(2,1)S(1)} %collective-permute-done.1.refs_1_.refs_5_, bf16[288,512]{1,0:T(8,128)(2,1)S(1)} %collective-permute-done.2.refs_2_.refs_6_, ...), custom_call_target="tpu_custom_call" | custom-call | flops 4000000000 | bytes 4194304 | tf_op jit(solution)/shard_map/forward1/pallas_call | solution.py:215
  69.8 3.6 %collective-permute-done.16.refs_3_.refs_11_ = bf16[256,512]{1,0:T(8,128)(2,1)S(1)} collective-permute-done((bf16[256,512]{1,0:T(8,128)(2,1)S(1)}, bf16[256,512]{1,0:T(8,128)(2,1)S(1)}, u32[]{:S(2)}, u32[]{:S(2)}) %collective-permute-start.16) | collective-permute-done | bytes 262176 | tf_op jit(solution)/shard_map/ppermute | solution.py:415
  74.8 3.6 %collective-permute-start.18 = (f32[12,1024]{1,0:T(8,128)S(1)}, f32[12,1024]{1,0:T(8,128)}, u32[]{:S(2)}, u32[]{:S(2)}) collective-permute-start(f32[12,1024]{1,0:T(8,128)S(1)} %weighted.1.refs_0_), channel_id=1, source_target_pairs={{0,8},{4,12},{8,0},{12,4},{1,9},{5,13},{9,1},{13,5},{2,10},{6,14},... | collective-permute-start | bytes 147464 | tf_op jit(solution)/shard_map/ppermute | solution.py:415
  78.4 2.3 %collective-permute-done.19.refs_3_ = f32[12,1024]{1,0:T(8,128)S(1)} collective-permute-done((f32[12,1024]{1,0:T(8,128)S(1)}, f32[12,1024]{1,0:T(8,128)S(1)}, u32[]{:S(2)}, u32[]{:S(2)}) %collective-permute-start.19) | collective-permute-done | bytes 49184 | tf_op jit(solution)/shard_map/ppermute | solution.py:415
  80.7 0.8 collective-permute-done.18.refs_2_
  81.5 1.2 collective-permute-done.17.refs_1_
  82.7 9.9 %backward1.1 = (f32[4,128,1024]{2,1,0:T(8,128)S(1)}, bf16[512,256]{1,0:T(8,128)(2,1)S(1)}, bf16[512,256]{1,0:T(8,128)(2,1)S(1)}) custom-call(s32[3]{0:T(128)S(1)} %pad_add_fusion.sc, f32[12,1024]{1,0:T(8,128)S(1)} %weighted.1.refs_0_, f32[12,1024]{1,0:T(8,128)} %collective-permute-done.17.refs_1_, f32[12,1024]{1,0:T(8,128)} %collective-permute-done.18.refs_2_, ...), custom_call_target="tpu_custom_call" | custom-call | flops 8000000000 | bytes 6291456 | tf_op jit(solution)/shard_map/backward1/pallas_call | solution.py:383
  92.7 1.3 copy-done.1
  94.0 3.0 %collective-permute-start.24 = (bf16[512,256]{1,0:T(8,128)(2,1)S(1)}, bf16[512,256]{1,0:T(8,128)(2,1)S(1)}, u32[]{:S(2)}, u32[]{:S(2)}) collective-permute-start(bf16[512,256]{1,0:T(8,128)(2,1)S(1)} %get-tuple-element.32), channel_id=1, source_target_pairs={{0,16},{16,32},{32,48},{48,64},{64,80},{80,96},{96,112},{112,0},{1... | collective-permute-start | bytes 786440 | tf_op jit(solution)/shard_map/ppermute | solution.py:415
  97.0 1.9 %collective-permute-start.25 = (bf16[512,256]{1,0:T(8,128)(2,1)S(1)}, bf16[512,256]{1,0:T(8,128)(2,1)S(1)}, u32[]{:S(2)}, u32[]{:S(2)}) collective-permute-start(bf16[512,256]{1,0:T(8,128)(2,1)S(1)} %get-tuple-element.33), channel_id=1, source_target_pairs={{0,112},{16,0},{32,16},{48,32},{64,48},{80,64},{96,80},{112,96},{1... | collective-permute-start | bytes 786440 | tf_op jit(solution)/shard_map/ppermute | solution.py:415
  98.9 13.3 %backward0.1 = (f32[256,512]{1,0:T(8,128)S(1)}, bf16[256,512]{1,0:T(8,128)(2,1)S(1)}, bf16[256,512]{1,0:T(8,128)(2,1)S(1)}, bf16[256,512]{1,0:T(8,128)(2,1)S(1)}...) custom-call(s32[3]{0:T(128)S(1)} %pad_add_fusion.sc, ...), custom_call_target="tpu_custom_call" | custom-call | flops 8000000000 | bytes 6291456 | tf_op jit(solution)/shard_map/backward0/pallas_call | solution.py:383
  112.3 5.4 %collective-permute-start.26 = (bf16[256,256]{1,0:T(8,128)(2,1)S(1)}, bf16[256,256]{1,0:T(8,128)(2,1)S(1)}, u32[]{:S(2)}, u32[]{:S(2)}) collective-permute-start(bf16[256,256]{1,0:T(8,128)(2,1)S(1)} %get-tuple-element.34), channel_id=1, source_target_pairs={{0,64},{16,80},{32,96},{48,112},{64,0},{80,16},{96,32},{112,48},{1... | collective-permute-start | bytes 393224 | tf_op jit(solution)/shard_map/ppermute | solution.py:415
  118.0 2.0 %collective-permute-start.21 = (bf16[256,512]{1,0:T(8,128)(2,1)S(1)}, bf16[256,512]{1,0:T(8,128)(2,1)S(1)}, u32[]{:S(2)}, u32[]{:S(2)}) collective-permute-start(bf16[256,512]{1,0:T(8,128)(2,1)S(1)} %get-tuple-element.29), channel_id=1, source_target_pairs={{0,8},{4,12},{8,0},{12,4},{1,9},{5,13},{9,1},{13,5},{2,10},{6,14},... | collective-permute-start | bytes 786440 | tf_op jit(solution)/shard_map/ppermute | solution.py:415
  119.9 1.0 collective-permute-start.22
  121.1 9.9 %collective-permute-done.20 = bf16[256,512]{1,0:T(8,128)(2,1)S(1)} collective-permute-done((bf16[256,512]{1,0:T(8,128)(2,1)S(1)}, bf16[256,512]{1,0:T(8,128)(2,1)S(1)}, u32[]{:S(2)}, u32[]{:S(2)}) %collective-permute-start.20) | collective-permute-done | bytes 262176 | tf_op jit(solution)/shard_map/ppermute | solution.py:415
  131.0 1.5 collective-permute-start.28
  132.6 1.0 collective-permute-start.23
  133.6 8.5 %collective-permute-done.28 = bf16[256,256]{1,0:T(8,128)(2,1)S(1)} collective-permute-done((bf16[256,256]{1,0:T(8,128)(2,1)S(1)}, bf16[256,256]{1,0:T(8,128)(2,1)S(1)}, u32[]{:S(2)}, u32[]{:S(2)}) %collective-permute-start.28) | collective-permute-done | bytes 131104 | tf_op jit(solution)/shard_map/ppermute | solution.py:415
  142.2 1.4 collective-permute-start.29
  144.0 0.8 maximum_select_fusion
  144.8 4.5 %collective-permute-done.29 = bf16[128,256]{1,0:T(8,128)(2,1)S(1)} collective-permute-done((bf16[128,256]{1,0:T(8,128)(2,1)S(1)}, bf16[128,256]{1,0:T(8,128)(2,1)S(1)}, u32[]{:S(2)}, u32[]{:S(2)}) %collective-permute-start.29) | collective-permute-done | bytes 65568 | tf_op jit(solution)/shard_map/ppermute | solution.py:420
  149.4 0.6 maximum_select_fusion.2
  150.0 0.6 maximum_select_fusion.1
  (49 shorter events, 4.4 us)
Async XLA Ops:
  0.6 34.6 %copy-start = (bf16[128,1024]{1,0:T(8,128)(2,1)S(1)}, bf16[128,1024]{1,0:T(8,128)(2,1)}, u32[]{:S(2)}) copy-start(bf16[128,1024]{1,0:T(8,128)(2,1)} %g0.1) | copy-start | bytes 786436
  3.4 12.9 %collective-permute-start.4 = (bf16[144,256]{1,0:T(8,128)(2,1)S(1)}, bf16[144,256]{1,0:T(8,128)(2,1)S(1)}, u32[]{:S(2)}, u32[]{:S(2)}) collective-permute-start(bf16[144,256]{1,0:T(8,128)(2,1)S(1)} %fusion.2), channel_id=1, source_target_pairs={{0,240},{16,224},{32,208},{48,192},{64,176},{80,160},{96,144},{112... | collective-permute-start | bytes 221192 | tf_op jit(solution)/shard_map/ppermute | solution.py:420
  11.0 10.8 %collective-permute-start = (bf16[144,512]{1,0:T(8,128)(2,1)S(1)}, bf16[144,512]{1,0:T(8,128)(2,1)S(1)}, u32[]{:S(2)}, u32[]{:S(2)}) collective-permute-start(bf16[144,512]{1,0:T(8,128)(2,1)S(1)} %concatenate.47), channel_id=1, source_target_pairs={{0,240},{16,224},{32,208},{48,192},{64,176},{80,160},{96,144},{112... | collective-permute-start | bytes 442376 | tf_op jit(solution)/shard_map/ppermute | solution.py:420
  11.1 21.0 %collective-permute-start.10 = (bf16[128,1024]{1,0:T(8,128)(2,1)}, bf16[128,1024]{1,0:T(8,128)(2,1)S(1)}, u32[]{:S(2)}, u32[]{:S(2)}) collective-permute-start(bf16[128,1024]{1,0:T(8,128)(2,1)} %g0.1), channel_id=1, source_target_pairs={{0,1},{1,0},{2,3},{3,2},{4,5},{5,4},{6,7},{7,6},{8,9},{9,8},{10,11... | collective-permute-start | bytes 786440 | tf_op jit(solution)/shard_map/ppermute | solution.py:415
  11.2 20.8 %collective-permute-start.11 = (bf16[128,1024]{1,0:T(8,128)(2,1)}, bf16[128,1024]{1,0:T(8,128)(2,1)S(1)}, u32[]{:S(2)}, u32[]{:S(2)}) collective-permute-start(bf16[128,1024]{1,0:T(8,128)(2,1)} %g0.1), channel_id=1, source_target_pairs={{0,2},{2,0},{1,3},{3,1},{4,6},{6,4},{5,7},{7,5},{8,10},{10,8},{9,1... | collective-permute-start | bytes 786440 | tf_op jit(solution)/shard_map/ppermute | solution.py:415
  17.0 10.3 %collective-permute-start.7 = (bf16[288,256]{1,0:T(8,128)(2,1)S(1)}, bf16[288,256]{1,0:T(8,128)(2,1)S(1)}, u32[]{:S(2)}, u32[]{:S(2)}) collective-permute-start(bf16[288,256]{1,0:T(8,128)(2,1)S(1)} %pad_maximum_fusion.4.refs_4_.refs_12_), channel_id=1, source_target_pairs={{0,32},{16,48},{32,64},{48,80},{64,96},{80,112},{96,0},{112,16},{1... | collective-permute-start | bytes 442376 | tf_op jit(solution)/shard_map/ppermute | solution.py:415
  18.0 12.5 %collective-permute-start.5 = (bf16[288,256]{1,0:T(8,128)(2,1)S(1)}, bf16[288,256]{1,0:T(8,128)(2,1)S(1)}, u32[]{:S(2)}, u32[]{:S(2)}) collective-permute-start(bf16[288,256]{1,0:T(8,128)(2,1)S(1)} %pad_maximum_fusion.4.refs_4_.refs_12_), channel_id=1, source_target_pairs={{0,96},{16,112},{32,0},{48,16},{64,32},{80,48},{96,64},{112,80},{1... | collective-permute-start | bytes 442376 | tf_op jit(solution)/shard_map/ppermute | solution.py:415
  21.9 25.5 %collective-permute-start.3 = (bf16[288,512]{1,0:T(8,128)(2,1)S(1)}, bf16[288,512]{1,0:T(8,128)(2,1)S(1)}, u32[]{:S(2)}, u32[]{:S(2)}) collective-permute-start(bf16[288,512]{1,0:T(8,128)(2,1)S(1)} %pad_maximum_fusion.refs_0_.refs_4_), channel_id=1, source_target_pairs={{0,4},{4,8},{8,12},{12,0},{1,5},{5,9},{9,13},{13,1},{2,6},{6,10},{... | collective-permute-start | bytes 884744 | tf_op jit(solution)/shard_map/ppermute | solution.py:415
  27.3 22.7 %collective-permute-start.2 = (bf16[288,512]{1,0:T(8,128)(2,1)S(1)}, bf16[288,512]{1,0:T(8,128)(2,1)S(1)}, u32[]{:S(2)}, u32[]{:S(2)}) collective-permute-start(bf16[288,512]{1,0:T(8,128)(2,1)S(1)} %pad_maximum_fusion.refs_0_.refs_4_), channel_id=1, source_target_pairs={{0,8},{4,12},{8,0},{12,4},{1,9},{5,13},{9,1},{13,5},{2,10},{6,14},... | collective-permute-start | bytes 884744 | tf_op jit(solution)/shard_map/ppermute | solution.py:415
  30.5 19.6 %collective-permute-start.1 = (bf16[288,512]{1,0:T(8,128)(2,1)S(1)}, bf16[288,512]{1,0:T(8,128)(2,1)S(1)}, u32[]{:S(2)}, u32[]{:S(2)}) collective-permute-start(bf16[288,512]{1,0:T(8,128)(2,1)S(1)} %pad_maximum_fusion.refs_0_.refs_4_), channel_id=1, source_target_pairs={{0,12},{4,0},{8,4},{12,8},{1,13},{5,1},{9,5},{13,9},{2,14},{6,2},{... | collective-permute-start | bytes 884744 | tf_op jit(solution)/shard_map/ppermute | solution.py:415
  32.0 6.5 %collective-permute-start.12 = (bf16[128,1024]{1,0:T(8,128)(2,1)S(1)}, bf16[128,1024]{1,0:T(8,128)(2,1)S(1)}, u32[]{:S(2)}, u32[]{:S(2)}) collective-permute-start(bf16[128,1024]{1,0:T(8,128)(2,1)S(1)} %collective-permute-done.11.g0), channel_id=1, source_target_pairs={{0,1},{1,0},{2,3},{3,2},{4,5},{5,4},{6,7},{7,6},{8,9},{9,8},{10,11... | collective-permute-start | bytes 786440 | tf_op jit(solution)/shard_map/ppermute | solution.py:415
  32.1 13.2 %collective-permute-start.6 = (bf16[288,256]{1,0:T(8,128)(2,1)S(1)}, bf16[288,256]{1,0:T(8,128)(2,1)S(1)}, u32[]{:S(2)}, u32[]{:S(2)}) collective-permute-start(bf16[288,256]{1,0:T(8,128)(2,1)S(1)} %pad_maximum_fusion.4.refs_4_.refs_12_), channel_id=1, source_target_pairs={{0,64},{16,80},{32,96},{48,112},{64,0},{80,16},{96,32},{112,48},{1... | collective-permute-start | bytes 442376 | tf_op jit(solution)/shard_map/ppermute | solution.py:415
  38.5 24.2 %collective-permute-start.9 = (bf16[576,256]{1,0:T(8,128)(2,1)S(1)}, bf16[576,256]{1,0:T(8,128)(2,1)S(1)}, u32[]{:S(2)}, u32[]{:S(2)}) collective-permute-start(bf16[576,256]{1,0:T(8,128)(2,1)S(1)} %get-tuple-element.41), channel_id=1, source_target_pairs={{0,16},{16,32},{32,48},{48,64},{64,80},{80,96},{96,112},{112,0},{1... | collective-permute-start | bytes 884744 | tf_op jit(solution)/shard_map/ppermute | solution.py:415
  45.3 17.4 %collective-permute-start.8 = (bf16[576,256]{1,0:T(8,128)(2,1)S(1)}, bf16[576,256]{1,0:T(8,128)(2,1)S(1)}, u32[]{:S(2)}, u32[]{:S(2)}) collective-permute-start(bf16[576,256]{1,0:T(8,128)(2,1)S(1)} %get-tuple-element.42), channel_id=1, source_target_pairs={{0,112},{16,0},{32,16},{48,32},{64,48},{80,64},{96,80},{112,96},{1... | collective-permute-start | bytes 884744 | tf_op jit(solution)/shard_map/ppermute | solution.py:415
  47.4 11.8 %collective-permute-start.13 = (bf16[128,512]{1,0:T(8,128)(2,1)S(1)}, bf16[128,512]{1,0:T(8,128)(2,1)S(1)}, u32[]{:S(2)}, u32[]{:S(2)}) collective-permute-start(bf16[128,512]{1,0:T(8,128)(2,1)S(1)} %get-tuple-element.25), channel_id=1, source_target_pairs={{0,240},{16,224},{32,208},{48,192},{64,176},{80,160},{96,144},{112... | collective-permute-start | bytes 393224 | tf_op jit(solution)/shard_map/ppermute | solution.py:420
  59.2 14.1 %collective-permute-start.16 = (bf16[256,512]{1,0:T(8,128)(2,1)S(1)}, bf16[256,512]{1,0:T(8,128)(2,1)S(1)}, u32[]{:S(2)}, u32[]{:S(2)}) collective-permute-start(bf16[256,512]{1,0:T(8,128)(2,1)S(1)} %constant_dynamic-update-slice_fusion.refs_0_.refs_8_), channel_id=1, source_target_pairs={{0,4},{4,8},{8,12},{12,0},{1,5},{5,9},{9,13},{13,1},{2,6},{6,10},{... | collective-permute-start | bytes 786440 | tf_op jit(solution)/shard_map/ppermute | solution.py:415
  59.5 13.9 %collective-permute-start.15 = (bf16[256,512]{1,0:T(8,128)(2,1)S(1)}, bf16[256,512]{1,0:T(8,128)(2,1)S(1)}, u32[]{:S(2)}, u32[]{:S(2)}) collective-permute-start(bf16[256,512]{1,0:T(8,128)(2,1)S(1)} %constant_dynamic-update-slice_fusion.refs_0_.refs_8_), channel_id=1, source_target_pairs={{0,8},{4,12},{8,0},{12,4},{1,9},{5,13},{9,1},{13,5},{2,10},{6,14},... | collective-permute-start | bytes 786440 | tf_op jit(solution)/shard_map/ppermute | solution.py:415
  61.8 12.1 %collective-permute-start.14 = (bf16[256,512]{1,0:T(8,128)(2,1)S(1)}, bf16[256,512]{1,0:T(8,128)(2,1)S(1)}, u32[]{:S(2)}, u32[]{:S(2)}) collective-permute-start(bf16[256,512]{1,0:T(8,128)(2,1)S(1)} %constant_dynamic-update-slice_fusion.refs_0_.refs_8_), channel_id=1, source_target_pairs={{0,12},{4,0},{8,4},{12,8},{1,13},{5,1},{9,5},{13,9},{2,14},{6,2},{... | collective-permute-start | bytes 786440 | tf_op jit(solution)/shard_map/ppermute | solution.py:415
  74.5 6.2 %collective-permute-start.19 = (f32[12,1024]{1,0:T(8,128)S(1)}, f32[12,1024]{1,0:T(8,128)S(1)}, u32[]{:S(2)}, u32[]{:S(2)}) collective-permute-start(f32[12,1024]{1,0:T(8,128)S(1)} %weighted.1.refs_0_), channel_id=1, source_target_pairs={{0,4},{4,8},{8,12},{12,0},{1,5},{5,9},{9,13},{13,1},{2,6},{6,10},{... | collective-permute-start | bytes 147464 | tf_op jit(solution)/shard_map/ppermute | solution.py:415
  74.8 6.7 %collective-permute-start.18 = (f32[12,1024]{1,0:T(8,128)S(1)}, f32[12,1024]{1,0:T(8,128)}, u32[]{:S(2)}, u32[]{:S(2)}) collective-permute-start(f32[12,1024]{1,0:T(8,128)S(1)} %weighted.1.refs_0_), channel_id=1, source_target_pairs={{0,8},{4,12},{8,0},{12,4},{1,9},{5,13},{9,1},{13,5},{2,10},{6,14},... | collective-permute-start | bytes 147464 | tf_op jit(solution)/shard_map/ppermute | solution.py:415
  78.4 4.4 %collective-permute-start.17 = (f32[12,1024]{1,0:T(8,128)S(1)}, f32[12,1024]{1,0:T(8,128)}, u32[]{:S(2)}, u32[]{:S(2)}) collective-permute-start(f32[12,1024]{1,0:T(8,128)S(1)} %weighted.1.refs_0_), channel_id=1, source_target_pairs={{0,12},{4,0},{8,4},{12,8},{1,13},{5,1},{9,5},{13,9},{2,14},{6,2},{... | collective-permute-start | bytes 147464 | tf_op jit(solution)/shard_map/ppermute | solution.py:415
  92.7 1.4 copy-start.1
  94.0 25.9 %collective-permute-start.24 = (bf16[512,256]{1,0:T(8,128)(2,1)S(1)}, bf16[512,256]{1,0:T(8,128)(2,1)S(1)}, u32[]{:S(2)}, u32[]{:S(2)}) collective-permute-start(bf16[512,256]{1,0:T(8,128)(2,1)S(1)} %get-tuple-element.32), channel_id=1, source_target_pairs={{0,16},{16,32},{32,48},{48,64},{64,80},{80,96},{96,112},{112,0},{1... | collective-permute-start | bytes 786440 | tf_op jit(solution)/shard_map/ppermute | solution.py:415
  97.0 23.9 %collective-permute-start.25 = (bf16[512,256]{1,0:T(8,128)(2,1)S(1)}, bf16[512,256]{1,0:T(8,128)(2,1)S(1)}, u32[]{:S(2)}, u32[]{:S(2)}) collective-permute-start(bf16[512,256]{1,0:T(8,128)(2,1)S(1)} %get-tuple-element.33), channel_id=1, source_target_pairs={{0,112},{16,0},{32,16},{48,32},{64,48},{80,64},{96,80},{112,96},{1... | collective-permute-start | bytes 786440 | tf_op jit(solution)/shard_map/ppermute | solution.py:415
  112.3 21.3 %collective-permute-start.26 = (bf16[256,256]{1,0:T(8,128)(2,1)S(1)}, bf16[256,256]{1,0:T(8,128)(2,1)S(1)}, u32[]{:S(2)}, u32[]{:S(2)}) collective-permute-start(bf16[256,256]{1,0:T(8,128)(2,1)S(1)} %get-tuple-element.34), channel_id=1, source_target_pairs={{0,64},{16,80},{32,96},{48,112},{64,0},{80,16},{96,32},{112,48},{1... | collective-permute-start | bytes 393224 | tf_op jit(solution)/shard_map/ppermute | solution.py:415
  117.7 13.3 %collective-permute-start.20 = (bf16[256,512]{1,0:T(8,128)(2,1)S(1)}, bf16[256,512]{1,0:T(8,128)(2,1)S(1)}, u32[]{:S(2)}, u32[]{:S(2)}) collective-permute-start(bf16[256,512]{1,0:T(8,128)(2,1)S(1)} %get-tuple-element.28), channel_id=1, source_target_pairs={{0,4},{4,8},{8,12},{12,0},{1,5},{5,9},{9,13},{13,1},{2,6},{6,10},{... | collective-permute-start | bytes 786440 | tf_op jit(solution)/shard_map/ppermute | solution.py:415
  118.0 14.5 %collective-permute-start.21 = (bf16[256,512]{1,0:T(8,128)(2,1)S(1)}, bf16[256,512]{1,0:T(8,128)(2,1)S(1)}, u32[]{:S(2)}, u32[]{:S(2)}) collective-permute-start(bf16[256,512]{1,0:T(8,128)(2,1)S(1)} %get-tuple-element.29), channel_id=1, source_target_pairs={{0,8},{4,12},{8,0},{12,4},{1,9},{5,13},{9,1},{13,5},{2,10},{6,14},... | collective-permute-start | bytes 786440 | tf_op jit(solution)/shard_map/ppermute | solution.py:415
  119.9 12.5 %collective-permute-start.22 = (bf16[256,512]{1,0:T(8,128)(2,1)S(1)}, bf16[256,512]{1,0:T(8,128)(2,1)S(1)}, u32[]{:S(2)}, u32[]{:S(2)}) collective-permute-start(bf16[256,512]{1,0:T(8,128)(2,1)S(1)} %get-tuple-element.30), channel_id=1, source_target_pairs={{0,12},{4,0},{8,4},{12,8},{1,13},{5,1},{9,5},{13,9},{2,14},{6,2},{... | collective-permute-start | bytes 786440 | tf_op jit(solution)/shard_map/ppermute | solution.py:415
  121.0 12.6 %collective-permute-start.27 = (bf16[256,256]{1,0:T(8,128)(2,1)S(1)}, bf16[256,256]{1,0:T(8,128)(2,1)S(1)}, u32[]{:S(2)}, u32[]{:S(2)}) collective-permute-start(bf16[256,256]{1,0:T(8,128)(2,1)S(1)} %add_convert_fusion.3), channel_id=1, source_target_pairs={{0,32},{16,48},{32,64},{48,80},{64,96},{80,112},{96,0},{112,16},{1... | collective-permute-start | bytes 393224 | tf_op jit(solution)/shard_map/ppermute | solution.py:415
  131.0 11.1 %collective-permute-start.28 = (bf16[256,256]{1,0:T(8,128)(2,1)S(1)}, bf16[256,256]{1,0:T(8,128)(2,1)S(1)}, u32[]{:S(2)}, u32[]{:S(2)}) collective-permute-start(bf16[256,256]{1,0:T(8,128)(2,1)S(1)} %add_convert_fusion.2), channel_id=1, source_target_pairs={{0,96},{16,112},{32,0},{48,16},{64,32},{80,48},{96,64},{112,80},{1... | collective-permute-start | bytes 393224 | tf_op jit(solution)/shard_map/ppermute | solution.py:415
  132.6 11.4 %collective-permute-start.23 = (bf16[128,512]{1,0:T(8,128)(2,1)S(1)}, bf16[128,512]{1,0:T(8,128)(2,1)S(1)}, u32[]{:S(2)}, u32[]{:S(2)}) collective-permute-start(bf16[128,512]{1,0:T(8,128)(2,1)S(1)} %get-tuple-element.38), channel_id=1, source_target_pairs={{0,240},{16,224},{32,208},{48,192},{64,176},{80,160},{96,144},{112... | collective-permute-start | bytes 393224 | tf_op jit(solution)/shard_map/ppermute | solution.py:420
  142.2 7.2 %collective-permute-start.29 = (bf16[128,256]{1,0:T(8,128)(2,1)S(1)}, bf16[128,256]{1,0:T(8,128)(2,1)S(1)}, u32[]{:S(2)}, u32[]{:S(2)}) collective-permute-start(bf16[128,256]{1,0:T(8,128)(2,1)S(1)} %slice.58), channel_id=1, source_target_pairs={{0,240},{16,224},{32,208},{48,192},{64,176},{80,160},{96,144},{112... | collective-permute-start | bytes 196616 | tf_op jit(solution)/shard_map/ppermute | solution.py:420
